TPU v7x, 512 devices: a whole 4x8x8 slice. The times are simulated.
512 devices in a mesh: seq: 128 (over z, y, x_hi), batch: 4 (over x_lo, core).
Axes of the slice: x: 4 (x_hi: 2, x_lo: 2; x = x_hi * 2 + x_lo), y: 8, z: 8, core: 2. Of those that a mesh axis runs over, the one named last changes fastest.
Arguments:
- tokens: bfloat16 [4, 262144, 128], P('batch', 'seq'), may hold values from -6 to 6
- grad_out: bfloat16 [4, 262144, 128], P('batch', 'seq'), may hold values from -6 to 6
- kernel: bfloat16 [512, 512, 128], P(None, 'seq'), may hold values from -6 to 6
- mix_inner: bfloat16 [512, 512], replicated, may hold values from -0.25 to 0.25
- mix_outer: bfloat16 [512, 512], replicated, may hold values from -0.25 to 0.25
- unmix_outer: bfloat16 [512, 512], replicated, may hold values from -0.25 to 0.25
- unmix_inner: bfloat16 [512, 512], replicated, may hold values from -0.25 to 0.25
Outputs:
- output: bfloat16 [4, 262144, 128], P('batch', 'seq')
- grad_tokens: bfloat16 [4, 262144, 128], P('batch', 'seq')
- grad_kernel: float32 [512, 512, 128], P(None, 'seq', 'batch')
All inputs are finite; a program needn't handle non-finite values.
Results may differ from a plain program's by a relative error of at most 0.018.
Values may be sent and summed in bfloat16 or wider, within the bound.
No kernel may reach another device: no remote copies, remote signals or barrier semaphores. Data moves between devices by JAX's collectives and lax.ppermute only.
A program may use at most 64 MiB of HBM per device.

v0:
```python
import jax
import jax.numpy as jnp
from jax import lax
from jax.sharding import PartitionSpec as P


def product(pattern, left, right):
    return jnp.einsum(pattern, left, right, preferred_element_type=jnp.float32).astype(jnp.bfloat16)


def body(tokens, grad_out, kernel, mix_inner, mix_outer, unmix_outer, unmix_inner):
    batch_rows, local_len, channels = tokens.shape
    block_len = mix_inner.shape[0]
    slab = local_len // block_len
    tok_grid = tokens.reshape(batch_rows, slab, block_len, channels)
    cot_grid = grad_out.reshape(batch_rows, slab, block_len, channels)
    inner_mixed = product("sabc,bk->sakc", tok_grid, mix_inner)
    grad_inner = product("snjc,kj->snkc", cot_grid, unmix_inner)
    spectrum = product(
        "sakc,am->smkc",
        lax.all_to_all(inner_mixed, "seq", split_axis=2, concat_axis=1, tiled=True),
        mix_outer,
    )
    grad_filtered = product(
        "snkc,mn->smkc",
        lax.all_to_all(grad_inner, "seq", split_axis=2, concat_axis=1, tiled=True),
        unmix_outer,
    )
    kernel_f = kernel.astype(jnp.float32)
    spec_f = spectrum.astype(jnp.float32)
    gradf_f = grad_filtered.astype(jnp.float32)
    filtered = (kernel_f * spec_f).astype(jnp.bfloat16)
    grad_spectrum = (kernel_f * gradf_f).astype(jnp.bfloat16)
    kernel_terms = jnp.sum(spec_f * gradf_f, axis=0)
    grad_kernel = lax.psum_scatter(kernel_terms, "batch", scatter_dimension=2, tiled=True)
    outer_done = product("smkc,mn->snkc", filtered, unmix_outer)
    grad_outer = product("smkc,am->sakc", grad_spectrum, mix_outer)
    result = product(
        "snkc,kj->snjc",
        lax.all_to_all(outer_done, "seq", split_axis=1, concat_axis=2, tiled=True),
        unmix_inner,
    )
    grad_tok = product(
        "sakc,bk->sabc",
        lax.all_to_all(grad_outer, "seq", split_axis=1, concat_axis=2, tiled=True),
        mix_inner,
    )
    output = result.reshape(batch_rows, local_len, channels)
    grad_tokens = grad_tok.reshape(batch_rows, local_len, channels)
    return (output, grad_tokens, grad_kernel)


def solution(mesh):
    return jax.shard_map(
        body,
        mesh=mesh,
        in_specs=(
            P("batch", "seq", None),
            P("batch", "seq", None),
            P(None, "seq", None),
            P(),
            P(),
            P(),
            P(),
        ),
        out_specs=(P("batch", "seq", None), P("batch", "seq", None), P(None, "seq", "batch")),
        check_vma=False,
    )
```

profile of v0, /device:TPU:8, one launch (start us, length us, event | category | flops | bytes accessed | tf_op | source)
XLA Modules:
  0.0 146.1 jit_solution(6068701418772457395)
XLA Ops:
  7.2 1.7 %fusion.4 = bf16[1,4,512,128]{3,2,1,0:T(8,128)(2,1)S(1)} fusion(bf16[4,512,128]{2,1,0:T(8,128)(2,1)} %bitcast.92, bf16[512,512]{1,0:T(8,128)(2,1)} %param.10), kind=kOutput, calls=%fused_computation.14 | convolution fusion | flops 268697600 | bytes 1572864 | tf_op jit(solution)/shard_map/sabc,bk->sakc/dot_general | solution.py:8
  8.9 1.2 copy.32
  10.1 20.0 %all-to-all-start = ((bf16[1,4,512,128]{3,1,0,2:T(4,128)(2,1)}), bf16[1,4,512,128]{3,1,0,2:T(4,128)(2,1)S(1)}, u32[]{:S(2)}, u32[]{:S(2)}) async-start(bf16[1,4,512,128]{3,1,0,2:T(4,128)(2,1)} %copy.32), calls=%async_computation | async-start | bytes 1048576 | tf_op jit(solution)/shard_map/all_to_all | solution.py:21
  30.5 1.2 copy.40
  31.7 19.9 %all-to-all-done = bf16[1,4,512,128]{3,1,0,2:T(4,128)(2,1)S(1)} async-done(((bf16[1,4,512,128]{3,1,0,2:T(4,128)(2,1)}), bf16[1,4,512,128]{3,1,0,2:T(4,128)(2,1)S(1)}, u32[]{:S(2)}, u32[]{:S(2)}) %all-to-all-start) | async-done | bytes 524320 | tf_op jit(solution)/shard_map/all_to_all | solution.py:21
  51.6 6.1 %all-to-all-start.2 = ((bf16[1,4,512,128]{3,1,0,2:T(4,128)(2,1)}), bf16[1,4,512,128]{3,1,0,2:T(4,128)(2,1)S(1)}, u32[]{:S(2)}, u32[]{:S(2)}) async-start(bf16[1,4,512,128]{3,1,0,2:T(4,128)(2,1)} %copy.40), calls=%async_computation.2 | async-start | bytes 1048576 | tf_op jit(solution)/shard_map/all_to_all | solution.py:26
  58.0 1.0 copy.33
  59.0 20.2 %all-to-all-done.2 = bf16[1,4,512,128]{3,1,0,2:T(4,128)(2,1)S(1)} async-done(((bf16[1,4,512,128]{3,1,0,2:T(4,128)(2,1)}), bf16[1,4,512,128]{3,1,0,2:T(4,128)(2,1)S(1)}, u32[]{:S(2)}, u32[]{:S(2)}) %all-to-all-start.2) | async-done | bytes 524320 | tf_op jit(solution)/shard_map/all_to_all | solution.py:26
  79.4 0.9 copy-done.3
  80.2 0.5 fusion.3
  81.2 1.1 copy.43
  82.3 6.6 %all-to-all-start.3 = ((bf16[1,512,4,128]{3,2,0,1:T(4,128)(2,1)}), bf16[1,512,4,128]{3,2,0,1:T(4,128)(2,1)}, u32[]{:S(2)}, u32[]{:S(2)}) async-start(bf16[1,512,4,128]{3,2,0,1:T(4,128)(2,1)} %copy.43), calls=%async_computation.3 | async-start | bytes 1048576 | tf_op jit(solution)/shard_map/all_to_all | solution.py:45
  89.0 2.5 %fusion.22 = (f32[512,4,128]{0,2,1:T(8,128)}, f32[512,4,128]{0,2,1:T(8,128)S(1)}) fusion(f32[512,4,128]{0,2,1:T(8,128)S(1)} %fusion.3, bf16[512,4,128]{2,0,1:T(8,128)(2,1)} %bitcast.88, bf16[512,512]{1,0:T(8,128)(2,1)S(1)} %copy-done), kind=kOutput, calls=%fused_computation.30 | convolution fusion | flops 269221888 | bytes 4194304 | tf_op jit(solution)/shard_map/sakc,am->smkc/dot_general | solution.py:8
  91.5 1.0 copy-done.4
  93.0 1.1 copy.35
  94.0 15.9 %all-to-all-done.3 = bf16[1,512,4,128]{3,2,0,1:T(4,128)(2,1)} async-done(((bf16[1,512,4,128]{3,2,0,1:T(4,128)(2,1)}), bf16[1,512,4,128]{3,2,0,1:T(4,128)(2,1)}, u32[]{:S(2)}, u32[]{:S(2)}) %all-to-all-start.3) | async-done | bytes 524320 | tf_op jit(solution)/shard_map/all_to_all | solution.py:45
  109.9 6.1 %all-to-all-start.1 = ((bf16[1,512,4,128]{3,2,0,1:T(4,128)(2,1)}), bf16[1,512,4,128]{3,2,0,1:T(4,128)(2,1)S(1)}, u32[]{:S(2)}, u32[]{:S(2)}) async-start(bf16[1,512,4,128]{3,2,0,1:T(4,128)(2,1)} %copy.35), calls=%async_computation.1 | async-start | bytes 1048576 | tf_op jit(solution)/shard_map/all_to_all | solution.py:40
  116.1 1.1 copy.44
  117.6 0.6 copy-done.6
  118.2 0.5 fusion.9
  118.7 1.0 copy.47
  119.7 17.0 %all-to-all-done.1 = bf16[1,512,4,128]{3,2,0,1:T(4,128)(2,1)S(1)} async-done(((bf16[1,512,4,128]{3,2,0,1:T(4,128)(2,1)}), bf16[1,512,4,128]{3,2,0,1:T(4,128)(2,1)S(1)}, u32[]{:S(2)}, u32[]{:S(2)}) %all-to-all-start.1) | async-done | bytes 524320 | tf_op jit(solution)/shard_map/all_to_all | solution.py:40
  137.2 0.6 copy-done.2
  138.3 1.0 copy.39
  (24 shorter events, 3.3 us)
Async XLA Ops:
  7.2 73.6 %copy-start = (bf16[512,512]{1,0:T(8,128)(2,1)S(1)}, bf16[512,512]{1,0:T(8,128)(2,1)}, u32[]{:S(2)}) copy-start(bf16[512,512]{1,0:T(8,128)(2,1)} %param.11) | copy-start | bytes 1572868
  10.1 20.0 %copy-start.1 = (bf16[512,512]{1,0:T(8,128)(2,1)S(1)}, bf16[512,512]{1,0:T(8,128)(2,1)}, u32[]{:S(2)}) copy-start(bf16[512,512]{1,0:T(8,128)(2,1)} %param.13) | copy-start | bytes 1572868
  10.1 20.0 %copy-start.5 = (bf16[1,2048,128]{2,1,0:T(8,128)(2,1)S(1)}, bf16[1,2048,128]{2,1,0:T(8,128)(2,1)}, u32[]{:S(2)}) copy-start(bf16[1,2048,128]{2,1,0:T(8,128)(2,1)} %param.8) | copy-start | bytes 1572868
  10.1 41.5 %all-to-all-start = ((bf16[1,4,512,128]{3,1,0,2:T(4,128)(2,1)}), bf16[1,4,512,128]{3,1,0,2:T(4,128)(2,1)S(1)}, u32[]{:S(2)}, u32[]{:S(2)}) async-start(bf16[1,4,512,128]{3,1,0,2:T(4,128)(2,1)} %copy.32), calls=%async_computation | async-start | bytes 1048576 | tf_op jit(solution)/shard_map/all_to_all | solution.py:21
  31.7 26.0 %copy-start.7 = (bf16[512,4,128]{2,1,0:T(4,128)(2,1)S(1)}, bf16[512,4,128]{2,1,0:T(4,128)(2,1)}, u32[]{:S(2)}) copy-start(bf16[512,4,128]{2,1,0:T(4,128)(2,1)} %param.9) | copy-start | bytes 1572868
  51.6 27.6 %all-to-all-start.2 = ((bf16[1,4,512,128]{3,1,0,2:T(4,128)(2,1)}), bf16[1,4,512,128]{3,1,0,2:T(4,128)(2,1)S(1)}, u32[]{:S(2)}, u32[]{:S(2)}) async-start(bf16[1,4,512,128]{3,1,0,2:T(4,128)(2,1)} %copy.40), calls=%async_computation.2 | async-start | bytes 1048576 | tf_op jit(solution)/shard_map/all_to_all | solution.py:26
  79.2 1.0 copy-start.3
  82.3 27.7 %all-to-all-start.3 = ((bf16[1,512,4,128]{3,2,0,1:T(4,128)(2,1)}), bf16[1,512,4,128]{3,2,0,1:T(4,128)(2,1)}, u32[]{:S(2)}, u32[]{:S(2)}) async-start(bf16[1,512,4,128]{3,2,0,1:T(4,128)(2,1)} %copy.43), calls=%async_computation.3 | async-start | bytes 1048576 | tf_op jit(solution)/shard_map/all_to_all | solution.py:45
  88.9 50.3 %reduce-scatter.2.cloned.1.call-start = ((), (), s32[]{:S(2)}) async-start(), calls=%async_computation.5 | async-start | bytes 1310720 | tf_op jit(solution)/shard_map/reduce_scatter | solution.py:35
  91.5 1.0 copy-start.4
  109.9 26.8 %all-to-all-start.1 = ((bf16[1,512,4,128]{3,2,0,1:T(4,128)(2,1)}), bf16[1,512,4,128]{3,2,0,1:T(4,128)(2,1)S(1)}, u32[]{:S(2)}, u32[]{:S(2)}) async-start(bf16[1,512,4,128]{3,2,0,1:T(4,128)(2,1)} %copy.35), calls=%async_computation.1 | async-start | bytes 1048576 | tf_op jit(solution)/shard_map/all_to_all | solution.py:40
  117.2 1.0 copy-start.6
  136.8 1.0 copy-start.2
Sparse Core Ops, SparseCore 0:
  93.2 27.1 reduce-scatter.1
where the time goes:
time: 147 us; the launch traced here: 146 us
  waiting for transfers between devices  73 us (50%)
  starting transfers between devices  38.8 us (26%)
  between operations  14.2 us (10%)
  local copies, waits for them, and re-layouts  13.1 us (9%)
  matrix products  6.99 us (5%)
    all_to_all x1, waiting for transfers between devices, body(): lax.all_to_all(grad_inner, 'seq', split_axis=2, concat_axis=1, tiled=True)  20.2 us
    all_to_all x1, starting transfers between devices, body(): lax.all_to_all(inner_mixed, 'seq', split_axis=2, concat_axis=1, tiled=True)  20 us
    all_to_all x1, waiting for transfers between devices, body(): lax.all_to_all(inner_mixed, 'seq', split_axis=2, concat_axis=1, tiled=True)  19.9 us
    all_to_all x1, waiting for transfers between devices, body(): lax.all_to_all(outer_done, 'seq', split_axis=1, concat_axis=2, tiled=True)  17 us
    all_to_all x1, waiting for transfers between devices, body(): lax.all_to_all(grad_outer, 'seq', split_axis=1, concat_axis=2, tiled=True)  15.9 us
    dot_general x8, matrix products, product(): jnp.einsum(pattern, left, right, preferred_element_type=jnp.float32)  6.99 us
    all_to_all x1, starting transfers between devices, body(): lax.all_to_all(grad_outer, 'seq', split_axis=1, concat_axis=2, tiled=True)  6.65 us
    convert_element_type x6, local copies, waits for them, and re-layouts, product(): jnp.einsum(pattern, left, right, preferred_element_type=jnp.float32)  6.53 us
  transfers between devices with their start and end apart: 5, of which 4 were waited for; matrix products, arithmetic and copies ran while one was open for 8% of the time, Pallas kernels for 0%

commit v1 on v0

v1 whole, which is shorter than its diff:
```python
import jax
import jax.numpy as jnp
from jax import lax
from jax.sharding import PartitionSpec as P


def product(pattern, left, right):
    return jnp.einsum(pattern, left, right, preferred_element_type=jnp.float32).astype(jnp.bfloat16)


def batch_sum(terms):
    outer, inner, channels = terms.shape
    quarter = channels // 4
    place = lax.axis_index("batch")
    core, side = lax.rem(place, 2), lax.div(place, 2)
    parts = terms.reshape(outer, inner, 2, 2, quarter)
    mine = lax.dynamic_index_in_dim(parts, core, 3, keepdims=False)
    other = lax.dynamic_index_in_dim(parts, 1 - core, 3, keepdims=False).astype(jnp.bfloat16)
    got = lax.ppermute(other, "batch", [(0, 1), (1, 0), (2, 3), (3, 2)])
    pair = mine + got.astype(jnp.float32)
    keep = lax.dynamic_index_in_dim(pair, side, 2, keepdims=False)
    give = lax.dynamic_index_in_dim(pair, 1 - side, 2, keepdims=False).astype(jnp.bfloat16)
    got = lax.ppermute(give, "batch", [(0, 2), (2, 0), (1, 3), (3, 1)])
    return keep + got.astype(jnp.float32)


def body(tokens, grad_out, kernel, mix_inner, mix_outer, unmix_outer, unmix_inner):
    local_len, channels = tokens.shape[1:]
    block_len = mix_inner.shape[0]
    slab = local_len // block_len
    groups = block_len // slab
    tok_grid = tokens.reshape(slab, block_len, channels)
    cot_grid = grad_out.reshape(slab, block_len, channels)
    inner_mixed = product("abc,bk->kac", tok_grid, mix_inner)
    grad_inner = product("njc,kj->knc", cot_grid, unmix_inner)
    sent = jnp.stack(
        [inner_mixed.reshape(groups, slab * slab, channels), grad_inner.reshape(groups, slab * slab, channels)], axis=1
    ).reshape(groups, 2 * slab * slab, channels)
    here = lax.all_to_all(sent, "seq", split_axis=0, concat_axis=0, tiled=True)
    here = here.reshape(groups, 2, slab, slab, channels)
    spectrum = product("gkac,gam->mkc", here[:, 0], mix_outer.reshape(groups, slab, block_len))
    grad_filtered = product("gknc,mgn->mkc", here[:, 1], unmix_outer.reshape(block_len, groups, slab))
    kernel_f = kernel.astype(jnp.float32)
    spec_f = spectrum.astype(jnp.float32)
    gradf_f = grad_filtered.astype(jnp.float32)
    filtered = (kernel_f * spec_f).astype(jnp.bfloat16)
    grad_spectrum = (kernel_f * gradf_f).astype(jnp.bfloat16)
    outer_done = product("mkc,mn->nkc", filtered, unmix_outer)
    grad_outer = product("mkc,am->akc", grad_spectrum, mix_outer)
    sent = jnp.stack(
        [outer_done.reshape(groups, slab * slab, channels), grad_outer.reshape(groups, slab * slab, channels)], axis=1
    ).reshape(groups, 2 * slab * slab, channels)
    back = lax.all_to_all(sent, "seq", split_axis=0, concat_axis=0, tiled=True)
    grad_kernel = batch_sum(spec_f * gradf_f)
    back = back.reshape(groups, 2, slab, slab, channels)
    result = product("gnkc,gkj->njc", back[:, 0], unmix_inner.reshape(groups, slab, block_len))
    grad_tok = product("gakc,bgk->abc", back[:, 1], mix_inner.reshape(block_len, groups, slab))
    return (result.reshape(1, local_len, channels), grad_tok.reshape(1, local_len, channels), grad_kernel)


def solution(mesh):
    return jax.shard_map(
        body,
        mesh=mesh,
        in_specs=(
            P("batch", "seq", None),
            P("batch", "seq", None),
            P(None, "seq", None),
            P(),
            P(),
            P(),
            P(),
        ),
        out_specs=(P("batch", "seq", None), P("batch", "seq", None), P(None, "seq", "batch")),
        check_vma=False,
    )
```

time: 147 us -> 114 us (0.78)
  waiting for transfers between devices: 73 us -> 51.5 us
  between operations: 14.2 us -> 0.96 us
  starting transfers between devices: 38.8 us -> 31.2 us
  local copies, waits for them, and re-layouts: 13.1 us -> 19.6 us
  matrix products: 6.99 us -> 8.71 us
    all_to_all x4 -> x2, waiting for transfers between devices: 72.9 us -> 45.3 us  [the longest x1 29 us: body(): here = lax.all_to_all(sent, 'seq', split_axis=0, concat_axis=0, tiled=True)]
    all_to_all x4 -> x2, starting transfers between devices: 38.8 us -> 26.6 us  [the longest x1 20 us: body(): here = lax.all_to_all(sent, 'seq', split_axis=0, concat_axis=0, tiled=True)]
    ppermute x0 -> x2, waiting for transfers between devices: none -> 6.21 us  [the longest x1 4.53 us: batch_sum(): got = lax.ppermute(give, 'batch', [(0, 2), (2, 0), (1, 3), (3, 1)])]
    ppermute x0 -> x2, starting transfers between devices: none -> 4.55 us  [the longest x1 2.64 us: batch_sum(): got = lax.ppermute(give, 'batch', [(0, 2), (2, 0), (1, 3), (3, 1)])]
    reshape x0 -> x6, local copies, waits for them, and re-layouts: none -> 4.46 us  [the longest x2 1.32 us: body(): mix_inner.reshape(block_len, groups, slab)]
    another operation x0 -> x2, local copies, waits for them, and re-layouts: none -> 2.33 us  [the longest x1 1.18 us: body(): jnp.stack([inner_mixed.reshape(groups, slab * slab, channels), grad_inner...]
    dot_general x8, matrix products: 6.99 us -> 8.71 us  [product(): jnp.einsum(pattern, left, right, preferred_element_type=jnp.float32)]
    unnamed x17 -> x35, local copies, waits for them, and re-layouts: 3.46 us -> 4.86 us
  transfers between devices with their start and end apart: 5 -> 4, of which waited for: 4 -> 4; matrix products, arithmetic and copies ran while one was open for 8% -> 6% of each run, Pallas kernels for 0% -> 0%
where the time goes in v1:
time: 114 us; the launch traced here: 113 us
  waiting for transfers between devices  51.5 us (45%)
  starting transfers between devices  31.2 us (27%)
  local copies, waits for them, and re-layouts  19.6 us (17%)
  matrix products  8.71 us (8%)
    all_to_all x1, waiting for transfers between devices, body(): here = lax.all_to_all(sent, 'seq', split_axis=0, concat_axis=0, tiled=True)  29 us
    all_to_all x1, starting transfers between devices, body(): here = lax.all_to_all(sent, 'seq', split_axis=0, concat_axis=0, tiled=True)  20 us
    all_to_all x1, waiting for transfers between devices, body(): back = lax.all_to_all(sent, 'seq', split_axis=0, concat_axis=0, tiled=True)  16.3 us
    dot_general x8, matrix products, product(): jnp.einsum(pattern, left, right, preferred_element_type=jnp.float32)  8.71 us
    all_to_all x1, starting transfers between devices, body(): back = lax.all_to_all(sent, 'seq', split_axis=0, concat_axis=0, tiled=True)  6.66 us
    convert_element_type x6, local copies, waits for them, and re-layouts, product(): jnp.einsum(pattern, left, right, preferred_element_type=jnp.float32)  5.23 us
    unnamed x35, local copies, waits for them, and re-layouts  4.86 us
    ppermute x1, waiting for transfers between devices, batch_sum(): got = lax.ppermute(give, 'batch', [(0, 2), (2, 0), (1, 3), (3, 1)])  4.53 us
  transfers between devices with their start and end apart: 4, of which 4 were waited for; matrix products, arithmetic and copies ran while one was open for 6% of the time, Pallas kernels for 0%

profile of v1, /device:TPU:8, one launch (start us, length us, event | category | flops | bytes accessed | tf_op | source)
XLA Modules:
  0.0 112.9 jit_solution(9263237178370471254)
XLA Ops:
  0.6 1.0 copy-done
  1.7 1.5 %convolution_convert_fusion.2 = bf16[512,4,128]{2,0,1:T(8,128)(2,1)S(1)} fusion(bf16[4,512,128]{2,1,0:T(8,128)(2,1)S(1)} %bitcast.111, bf16[512,512]{1,0:T(8,128)(2,1)} %param.13), kind=kOutput, calls=%fused_computation.8 | convolution fusion | flops 268697600 | bytes 1572864 | tf_op jit(solution)/shard_map/njc,kj->knc/dot_general | solution.py:8
  5.4 1.2 %copy.38 = bf16[128,2,16,128]{3,2,1,0:T(8,128)(2,1)} copy(bf16[128,2,16,128]{3,2,0,1:T(8,128)(2,1)S(1)} %pad_maximum_fusion) | data formatting | bytes 2097152 | tf_op jit(solution)/shard_map/stack | solution.py:36
  6.5 20.0 %all-to-all-start = ((bf16[128,32,128]{2,1,0:T(8,128)(2,1)}), bf16[128,32,128]{2,1,0:T(8,128)(2,1)S(1)}, u32[]{:S(2)}, u32[]{:S(2)}) async-start(bf16[128,32,128]{2,1,0:T(8,128)(2,1)} %bitcast.6), calls=%async_computation | async-start | bytes 2097152 | tf_op jit(solution)/shard_map/all_to_all | solution.py:39
  26.9 1.2 %copy.43 = bf16[512,128,4]{1,0,2:T(8,128)(2,1)} copy(bf16[512,128,4]{0,2,1:T(4,128)(2,1)S(1)} %reshape.52) | data formatting | bytes 1048576 | tf_op jit(solution)/shard_map/reshape | solution.py:42
  29.1 0.9 reshape.51
  30.0 29.0 %all-to-all-done = bf16[128,32,128]{2,1,0:T(8,128)(2,1)S(1)} async-done(((bf16[128,32,128]{2,1,0:T(8,128)(2,1)}), bf16[128,32,128]{2,1,0:T(8,128)(2,1)S(1)}, u32[]{:S(2)}, u32[]{:S(2)}) %all-to-all-start) | async-done | bytes 1048608 | tf_op jit(solution)/shard_map/all_to_all | solution.py:39
  59.0 1.0 copy.39
  60.0 1.6 %fusion.5 = f32[512,4,128]{0,2,1:T(8,128)S(1)} fusion(bf16[128,2,4,4,128]{0,4,3,2,1:T(8,128)(2,1)S(1)} %bitcast.112, bf16[512,128,4]{1,0,2:T(8,128)(2,1)} %copy.43), kind=kOutput, calls=%fused_computation.15 | convolution fusion | flops 268959744 | bytes 2097152 | tf_op jit(solution)/shard_map/gknc,mgn->mkc/dot_general | solution.py:8
  61.6 1.3 %fusion.11 = bf16[512,4,128]{0,2,1:T(8,128)(2,1)} fusion(f32[512,4,128]{0,2,1:T(8,128)S(1)} %fusion.5, bf16[512,4,128]{0,2,1:T(8,128)(2,1)S(1)} %copy.34, bf16[512,512]{1,0:T(8,128)(2,1)S(1)} %copy-done.3), kind=kOutput, calls=%fused_computation.21 | convolution fusion | flops 269484032 | bytes 2621440 | tf_op jit(solution)/shard_map/mkc,am->akc/dot_general | solution.py:8
  62.9 2.1 %copy.44 = bf16[512,4,128]{2,1,0:T(4,128)(2,1)} copy(bf16[512,4,128]{0,2,1:T(8,128)(2,1)} %fusion.11) | data formatting | bytes 1048576 | tf_op jit(solution)/shard_map/convert_element_type | solution.py:8
  65.0 2.6 %fusion.28 = (f32[512,4,128]{0,2,1:T(8,128)}, f32[512,4,128]{0,2,1:T(8,128)S(1)}) fusion(f32[512,4,128]{0,2,1:T(8,128)S(1)} %fusion.5, bf16[128,4,512]{2,1,0:T(4,128)(2,1)} %reshape.51, bf16[128,2,4,4,128]{0,4,3,2,1:T(8,128)(2,1)S(1)} %bitcast.113), kind=kOutput, calls=%fused_computation.48 | convolution fusion | flops 269221888 | bytes 4194304 | tf_op jit(solution)/shard_map/gkac,gam->mkc/dot_general | solution.py:8
  69.1 1.2 %copy.45 = bf16[128,2,16,128]{3,2,1,0:T(8,128)(2,1)} copy(bf16[128,2,16,128]{3,2,0,1:T(8,128)(2,1)S(1)} %pad_maximum_fusion.1) | data formatting | bytes 2097152 | tf_op jit(solution)/shard_map/stack | solution.py:50
  70.3 6.7 %all-to-all-start.1 = ((bf16[128,32,128]{2,1,0:T(8,128)(2,1)}), bf16[128,32,128]{2,1,0:T(8,128)(2,1)S(1)}, u32[]{:S(2)}, u32[]{:S(2)}) async-start(bf16[128,32,128]{2,1,0:T(8,128)(2,1)} %bitcast.24), calls=%async_computation.1 | async-start | bytes 2097152 | tf_op jit(solution)/shard_map/all_to_all | solution.py:53
  77.7 1.9 %collective-permute-start = (bf16[512,4,2,32]{0,3,1,2:T(8,128)(2,1)}, bf16[512,4,2,32]{0,3,1,2:T(8,128)(2,1)S(1)}, u32[]{:S(2)}, u32[]{:S(2)}) collective-permute-start(bf16[512,4,2,32]{0,3,1,2:T(8,128)(2,1)} %fusion.26), channel_id=1, source_target_pairs={{0,1},{1,0},{2,3},{3,2},{4,5},{5,4},{6,7},{7,6},{8,9},{9,8},{10,11... | collective-permute-start | bytes 786440 | tf_op jit(solution)/shard_map/ppermute | solution.py:19
  79.6 1.7 %collective-permute-done = bf16[512,4,2,32]{0,3,1,2:T(8,128)(2,1)S(1)} collective-permute-done((bf16[512,4,2,32]{0,3,1,2:T(8,128)(2,1)}, bf16[512,4,2,32]{0,3,1,2:T(8,128)(2,1)S(1)}, u32[]{:S(2)}, u32[]{:S(2)}) %collective-permute-start) | collective-permute-done | bytes 262176 | tf_op jit(solution)/shard_map/ppermute | solution.py:19
  82.2 2.6 %collective-permute-start.1 = (bf16[512,4,32]{0,2,1:T(8,128)(2,1)S(1)}, bf16[512,4,32]{0,2,1:T(8,128)(2,1)S(1)}, u32[]{:S(2)}, u32[]{:S(2)}) collective-permute-start(bf16[512,4,32]{0,2,1:T(8,128)(2,1)S(1)} %fusion.27), channel_id=1, source_target_pairs={{0,2},{2,0},{1,3},{3,1},{4,6},{6,4},{5,7},{7,5},{8,10},{10,8},{9,1... | collective-permute-start | bytes 393224 | tf_op jit(solution)/shard_map/ppermute | solution.py:23
  84.9 0.9 reshape.55
  86.2 1.2 %copy.50 = bf16[512,128,4]{1,0,2:T(8,128)(2,1)} copy(bf16[512,128,4]{0,2,1:T(4,128)(2,1)S(1)} %reshape.57) | data formatting | bytes 1048576 | tf_op jit(solution)/shard_map/reshape | solution.py:57
  87.4 4.5 %collective-permute-done.1 = bf16[512,4,32]{0,2,1:T(8,128)(2,1)S(1)} collective-permute-done((bf16[512,4,32]{0,2,1:T(8,128)(2,1)S(1)}, bf16[512,4,32]{0,2,1:T(8,128)(2,1)S(1)}, u32[]{:S(2)}, u32[]{:S(2)}) %collective-permute-start.1) | collective-permute-done | bytes 131104 | tf_op jit(solution)/shard_map/ppermute | solution.py:23
  92.6 16.3 %all-to-all-done.1 = bf16[128,32,128]{2,1,0:T(8,128)(2,1)S(1)} async-done(((bf16[128,32,128]{2,1,0:T(8,128)(2,1)}), bf16[128,32,128]{2,1,0:T(8,128)(2,1)S(1)}, u32[]{:S(2)}, u32[]{:S(2)}) %all-to-all-start.1) | async-done | bytes 1048608 | tf_op jit(solution)/shard_map/all_to_all | solution.py:53
  109.0 1.0 copy.46
  110.4 1.0 copy.48
  111.9 1.0 copy.51
  (49 shorter events, 8.8 us)
Async XLA Ops:
  0.6 1.0 copy-start
  3.2 1.0 copy-start.11
  3.2 1.2 %copy-start.15 = (bf16[1,2048,128]{2,1,0:T(8,128)(2,1)S(1)}, bf16[1,2048,128]{2,1,0:T(8,128)(2,1)}, u32[]{:S(2)}) copy-start(bf16[1,2048,128]{2,1,0:T(8,128)(2,1)} %param.7) | copy-start | bytes 1572868
  6.5 20.0 %copy-start.4 = (bf16[512,512]{1,0:T(8,128)(2,1)S(1)}, bf16[512,512]{1,0:T(8,128)(2,1)}, u32[]{:S(2)}) copy-start(bf16[512,512]{1,0:T(8,128)(2,1)} %param.12) | copy-start | bytes 1572868
  6.5 52.5 %all-to-all-start = ((bf16[128,32,128]{2,1,0:T(8,128)(2,1)}), bf16[128,32,128]{2,1,0:T(8,128)(2,1)S(1)}, u32[]{:S(2)}, u32[]{:S(2)}) async-start(bf16[128,32,128]{2,1,0:T(8,128)(2,1)} %bitcast.6), calls=%async_computation | async-start | bytes 2097152 | tf_op jit(solution)/shard_map/all_to_all | solution.py:39
  26.9 1.2 %copy-start.10 = (bf16[512,4,128]{2,1,0:T(4,128)(2,1)S(1)}, bf16[512,4,128]{2,1,0:T(4,128)(2,1)}, u32[]{:S(2)}) copy-start(bf16[512,4,128]{2,1,0:T(4,128)(2,1)} %param.9) | copy-start | bytes 1572868
  28.1 1.0 copy-start.2
  60.0 1.6 %copy-start.3 = (bf16[512,512]{1,0:T(8,128)(2,1)S(1)}, bf16[512,512]{1,0:T(8,128)(2,1)}, u32[]{:S(2)}) copy-start(bf16[512,512]{1,0:T(8,128)(2,1)} %param.11) | copy-start | bytes 1572868
  65.0 2.6 %copy-start.5 = (bf16[512,512]{1,0:T(8,128)(2,1)S(1)}, bf16[512,512]{1,0:T(8,128)(2,1)}, u32[]{:S(2)}) copy-start(bf16[512,512]{1,0:T(8,128)(2,1)} %param.12) | copy-start | bytes 1572868
  68.0 1.0 copy-start.7
  70.3 6.7 %copy-start.1 = (f32[512,4,128]{0,2,1:T(8,128)S(1)}, f32[512,4,128]{0,2,1:T(8,128)}, u32[]{:S(2)}) copy-start(f32[512,4,128]{0,2,1:T(8,128)} %get-tuple-element.3) | copy-start | bytes 3145732
  70.3 38.7 %all-to-all-start.1 = ((bf16[128,32,128]{2,1,0:T(8,128)(2,1)}), bf16[128,32,128]{2,1,0:T(8,128)(2,1)S(1)}, u32[]{:S(2)}, u32[]{:S(2)}) async-start(bf16[128,32,128]{2,1,0:T(8,128)(2,1)} %bitcast.24), calls=%async_computation.1 | async-start | bytes 2097152 | tf_op jit(solution)/shard_map/all_to_all | solution.py:53
  77.7 3.6 %collective-permute-start = (bf16[512,4,2,32]{0,3,1,2:T(8,128)(2,1)}, bf16[512,4,2,32]{0,3,1,2:T(8,128)(2,1)S(1)}, u32[]{:S(2)}, u32[]{:S(2)}) collective-permute-start(bf16[512,4,2,32]{0,3,1,2:T(8,128)(2,1)} %fusion.26), channel_id=1, source_target_pairs={{0,1},{1,0},{2,3},{3,2},{4,5},{5,4},{6,7},{7,6},{8,9},{9,8},{10,11... | collective-permute-start | bytes 786440 | tf_op jit(solution)/shard_map/ppermute | solution.py:19
  79.6 5.3 %copy-start.6 = (bf16[512,512]{1,0:T(8,128)(2,1)S(1)}, bf16[512,512]{1,0:T(8,128)(2,1)}, u32[]{:S(2)}) copy-start(bf16[512,512]{1,0:T(8,128)(2,1)} %param.13) | copy-start | bytes 1572868
  81.4 0.8 copy-start.8
  82.2 3.6 %copy-start.12 = (bf16[512,512]{1,0:T(8,128)(2,1)S(1)}, bf16[512,512]{1,0:T(8,128)(2,1)}, u32[]{:S(2)}) copy-start(bf16[512,512]{1,0:T(8,128)(2,1)} %param.10) | copy-start | bytes 1572868
  82.2 9.7 %collective-permute-start.1 = (bf16[512,4,32]{0,2,1:T(8,128)(2,1)S(1)}, bf16[512,4,32]{0,2,1:T(8,128)(2,1)S(1)}, u32[]{:S(2)}, u32[]{:S(2)}) collective-permute-start(bf16[512,4,32]{0,2,1:T(8,128)(2,1)S(1)} %fusion.27), channel_id=1, source_target_pairs={{0,2},{2,0},{1,3},{3,1},{4,6},{6,4},{5,7},{7,5},{8,10},{10,8},{9,1... | collective-permute-start | bytes 393224 | tf_op jit(solution)/shard_map/ppermute | solution.py:23
  86.2 5.7 %copy-start.9 = (f32[512,4,2,32]{0,3,1,2:T(8,128)S(1)}, f32[512,4,2,32]{0,3,1,2:T(8,128)}, u32[]{:S(2)}) copy-start(f32[512,4,2,32]{0,3,1,2:T(8,128)} %copy-done.8) | copy-start | bytes 1572868
  92.6 17.3 %copy-start.13 = (bf16[128,4,512]{2,1,0:T(4,128)(2,1)S(1)}, bf16[128,4,512]{2,1,0:T(4,128)(2,1)}, u32[]{:S(2)}) copy-start(bf16[128,4,512]{2,1,0:T(4,128)(2,1)} %reshape.55) | copy-start | bytes 1572868
  110.4 1.0 copy-start.14

commit v2 on v1

v2 whole, which is shorter than its diff:
```python
import functools

import jax
import jax.numpy as jnp
from jax import lax
from jax.experimental import pallas as pl
from jax.experimental.pallas import tpu as pltpu
from jax.sharding import PartitionSpec as P

VMEM_LIMIT = 24 * 1024 * 1024


def dot(left, right, left_dim=1):
    return lax.dot_general(left, right, (((left_dim,), (0,)), ((), ())), preferred_element_type=jnp.float32)


def scatter_rows(slab, product, scratch, out_ref, part):
    block, width = product.shape
    channels = width // slab
    for g in range(slab):
        scratch[pl.ds(g, block, stride=slab), :] = product[:, g * channels : (g + 1) * channels]
    rows = slab * slab
    out_ref[:, part * rows : (part + 1) * rows, :] = (
        scratch[...].astype(jnp.bfloat16).reshape(block // slab, rows, channels)
    )


def gather_rows(slab, groups, scratch, part):
    rows = slab * slab
    lanes = []
    for i in range(slab):
        pieces = [
            scratch[pl.ds(part * rows + i * slab + j, groups, stride=2 * rows), :].astype(jnp.bfloat16)
            for j in range(slab)
        ]
        lanes.append(jnp.concatenate(pieces, axis=0))
    return jnp.concatenate(lanes, axis=1)


def lanes_of(ref, slab):
    block = ref.shape[0] // slab
    return jnp.concatenate([ref[a * block : (a + 1) * block, :] for a in range(slab)], axis=1)


def before_kernel(slab, tok_ref, cot_ref, mix_ref, unmix_ref, out_ref, scratch):
    scatter_rows(slab, dot(mix_ref[...], lanes_of(tok_ref, slab), 0), scratch.at[0], out_ref, 0)
    scatter_rows(slab, dot(unmix_ref[...], lanes_of(cot_ref, slab)), scratch.at[1], out_ref, 1)


def between_kernel(slab, in_ref, ker_ref, mixt_ref, unmixp_ref, unmixt_ref, mix_ref, out_ref, term_ref, rows, scratch):
    groups = in_ref.shape[0]
    channels = in_ref.shape[2]
    rows[...] = in_ref[...].reshape(rows.shape).astype(jnp.float32)
    weight = ker_ref[...].astype(jnp.float32)
    spectrum = dot(mixt_ref[...], gather_rows(slab, groups, rows, 0)).astype(jnp.bfloat16).astype(jnp.float32)
    filtered = (weight * spectrum).astype(jnp.bfloat16)
    scatter_rows(slab, dot(unmixt_ref[...], filtered), scratch.at[0], out_ref, 0)
    gradf = dot(unmixp_ref[...], gather_rows(slab, groups, rows, 1)).astype(jnp.bfloat16).astype(jnp.float32)
    grad_spectrum = (weight * gradf).astype(jnp.bfloat16)
    scatter_rows(slab, dot(mix_ref[...], grad_spectrum), scratch.at[1], out_ref, 1)
    terms = spectrum * gradf
    for i in range(slab):
        term_ref[i] = terms[:, i * channels : (i + 1) * channels]


def after_kernel(slab, in_ref, unmixt_ref, mixp_ref, res_ref, tok_ref, rows):
    groups = in_ref.shape[0]
    channels = in_ref.shape[2]
    block = unmixt_ref.shape[0]
    rows[...] = in_ref[...].reshape(rows.shape).astype(jnp.float32)
    for part, (weight_ref, out_ref) in enumerate(((unmixt_ref, res_ref), (mixp_ref, tok_ref))):
        product = dot(weight_ref[...], gather_rows(slab, groups, rows, part)).astype(jnp.bfloat16)
        for i in range(slab):
            out_ref[i * block : (i + 1) * block, :] = product[:, i * channels : (i + 1) * channels]


def call(kernel, outs, scratch, *args):
    return pl.pallas_call(
        kernel,
        out_shape=outs,
        in_specs=[pl.BlockSpec(memory_space=pltpu.VMEM)] * len(args),
        out_specs=jax.tree.map(lambda _: pl.BlockSpec(memory_space=pltpu.VMEM), outs),
        scratch_shapes=scratch,
        compiler_params=pltpu.CompilerParams(vmem_limit_bytes=VMEM_LIMIT),
    )(*args)


def batch_sum(terms):
    inner, outer, channels = terms.shape
    quarter = channels // 4
    place = lax.axis_index("batch")
    core, side = lax.rem(place, 2), lax.div(place, 2)
    parts = terms.reshape(inner, outer, 2, 2, quarter)
    mine = lax.dynamic_index_in_dim(parts, core, 3, keepdims=False)
    other = lax.dynamic_index_in_dim(parts, 1 - core, 3, keepdims=False).astype(jnp.bfloat16)
    got = lax.ppermute(other, "batch", [(0, 1), (1, 0), (2, 3), (3, 2)])
    pair = mine + got.astype(jnp.float32)
    keep = lax.dynamic_index_in_dim(pair, side, 2, keepdims=False)
    give = lax.dynamic_index_in_dim(pair, 1 - side, 2, keepdims=False).astype(jnp.bfloat16)
    got = lax.ppermute(give, "batch", [(0, 2), (2, 0), (1, 3), (3, 1)])
    return (keep + got.astype(jnp.float32)).transpose(1, 0, 2)


def body(tokens, grad_out, kernel, mix_inner, mix_outer, unmix_outer, unmix_inner):
    local_len, channels = tokens.shape[1:]
    block = mix_inner.shape[0]
    slab = local_len // block
    groups = block // slab
    bf16, f32 = jnp.bfloat16, jnp.float32
    message = jax.ShapeDtypeStruct((groups, 2 * slab * slab, channels), bf16)
    stage = pltpu.VMEM((2, block * slab, channels), f32)
    rows = pltpu.VMEM((2 * block * slab, channels), f32)

    def columns(weight):
        return weight.reshape(block, groups, slab).transpose(0, 2, 1).reshape(block, block)

    sent = call(
        functools.partial(before_kernel, slab),
        message,
        [stage],
        tokens.reshape(local_len, channels),
        grad_out.reshape(local_len, channels),
        mix_inner,
        unmix_inner,
    )
    here = lax.all_to_all(sent, "seq", split_axis=0, concat_axis=0, tiled=True)
    sent, terms = call(
        functools.partial(between_kernel, slab),
        (message, jax.ShapeDtypeStruct((slab, block, channels), f32)),
        [rows, stage],
        here,
        kernel.reshape(block, slab * channels),
        columns(mix_outer.T),
        columns(unmix_outer),
        unmix_outer.T,
        mix_outer,
    )
    back = lax.all_to_all(sent, "seq", split_axis=0, concat_axis=0, tiled=True)
    grad_kernel = batch_sum(terms)
    flat = jax.ShapeDtypeStruct((local_len, channels), bf16)
    output, grad_tokens = call(
        functools.partial(after_kernel, slab),
        (flat, flat),
        [rows],
        back,
        columns(unmix_inner.T),
        columns(mix_inner),
    )
    return (output.reshape(1, local_len, channels), grad_tokens.reshape(1, local_len, channels), grad_kernel)


def solution(mesh):
    return jax.shard_map(
        body,
        mesh=mesh,
        in_specs=(
            P("batch", "seq", None),
            P("batch", "seq", None),
            P(None, "seq", None),
            P(),
            P(),
            P(),
            P(),
        ),
        out_specs=(P("batch", "seq", None), P("batch", "seq", None), P(None, "seq", "batch")),
        check_vma=False,
    )
```

time: 114 us -> 107 us (0.939)
  matrix products: 8.71 us -> 0 us
  Pallas kernels: 0 us -> 6.93 us
  local copies, waits for them, and re-layouts: 19.6 us -> 16.8 us
  waiting for transfers between devices: 51.5 us -> 49.3 us
    dot_general x8 -> x0, matrix products: 8.71 us -> none  [product(): jnp.einsum(pattern, left, right, preferred_element_type=jnp.float32)]
    pallas_call x0 -> x3, Pallas kernels: none -> 6.93 us  [call(): pl.pallas_call(kernel, out_shape=outs, in_specs=[pl.BlockSpec(memory_spac...]
    convert_element_type x6 -> x0, local copies, waits for them, and re-layouts: 5.23 us -> none  [product(): jnp.einsum(pattern, left, right, preferred_element_type=jnp.float32)]
    unnamed x35 -> x31, local copies, waits for them, and re-layouts: 4.86 us -> 8.64 us
    ppermute x1, waiting for transfers between devices: 4.53 us -> 7.47 us  [batch_sum(): got = lax.ppermute(give, 'batch', [(0, 2), (2, 0), (1, 3), (3, 1)])]
    all_to_all x1, waiting for transfers between devices: 29 us -> 26.4 us  [body(): here = lax.all_to_all(sent, 'seq', split_axis=0, concat_axis=0, tiled=True)]
    transpose x0 -> x2, local copies, waits for them, and re-layouts: none -> 2.46 us  [columns(): weight.reshape(block, groups, slab).transpose(0, 2, 1).reshape(block, block)]
    another operation x2 -> x0, local copies, waits for them, and re-layouts: 2.33 us -> none  [the longest x1 1.18 us: body(): jnp.stack([inner_mixed.reshape(groups, slab * slab, channels), grad_inner...]
  transfers between devices with their start and end apart: 4 -> 4, of which waited for: 4 -> 3; matrix products, arithmetic and copies ran while one was open for 6% -> 9% of each run, Pallas kernels for 0% -> 0%
where the time goes in v2:
time: 107 us; the launch traced here: 106 us
  waiting for transfers between devices  49.3 us (46%)
  starting transfers between devices  31.2 us (29%)
  local copies, waits for them, and re-layouts  16.8 us (16%)
  Pallas kernels  6.93 us (6%)
    all_to_all x1, waiting for transfers between devices, body(): here = lax.all_to_all(sent, 'seq', split_axis=0, concat_axis=0, tiled=True)  26.4 us
    all_to_all x1, starting transfers between devices, body(): here = lax.all_to_all(sent, 'seq', split_axis=0, concat_axis=0, tiled=True)  20 us
    all_to_all x1, waiting for transfers between devices, body(): back = lax.all_to_all(sent, 'seq', split_axis=0, concat_axis=0, tiled=True)  15.5 us
    unnamed x31, local copies, waits for them, and re-layouts  8.64 us
    ppermute x1, waiting for transfers between devices, batch_sum(): got = lax.ppermute(give, 'batch', [(0, 2), (2, 0), (1, 3), (3, 1)])  7.47 us
    pallas_call x3, Pallas kernels, call(): pl.pallas_call(kernel, out_shape=outs, in_specs=[pl.BlockSpec(memory_spac...  6.93 us
    all_to_all x1, starting transfers between devices, body(): back = lax.all_to_all(sent, 'seq', split_axis=0, concat_axis=0, tiled=True)  6.65 us
    reshape x8, local copies, waits for them, and re-layouts, columns(): weight.reshape(block, groups, slab).transpose(0, 2, 1).reshape(block, block)  4.59 us
  transfers between devices with their start and end apart: 4, of which 3 were waited for; matrix products, arithmetic and copies ran while one was open for 9% of the time, Pallas kernels for 0%

profile of v2, /device:TPU:8, one launch (start us, length us, event | category | flops | bytes accessed | tf_op | source)
XLA Modules:
  0.0 105.9 jit_solution(6350936983423167397)
XLA Ops:
  0.6 1.0 copy-done.2
  1.7 1.0 copy-done.4
  2.7 1.0 copy-done.9
  3.8 1.0 copy-done.10
  4.8 1.8 %shard_map.94 = bf16[128,32,128]{2,1,0:T(8,128)(2,1)} custom-call(bf16[2048,128]{1,0:T(8,128)(2,1)S(1)} %bitcast.52, bf16[2048,128]{1,0:T(8,128)(2,1)S(1)} %bitcast.53, bf16[512,512]{1,0:T(8,128)(2,1)S(1)} %copy-done.2, bf16[512,512]{1,0:T(8,128)(2,1)S(1)} %copy-done.4), custom_call_target="tpu_custom_call" | custom-call | tf_op jit(solution)/shard_map/pallas_call | solution.py:78
  6.6 20.0 %all-to-all-start = ((bf16[128,32,128]{2,1,0:T(8,128)(2,1)}), bf16[128,32,128]{2,1,0:T(8,128)(2,1)S(1)}, u32[]{:S(2)}, u32[]{:S(2)}) async-start(bf16[128,32,128]{2,1,0:T(8,128)(2,1)} %shard_map.94), calls=%async_computation | async-start | bytes 2097152 | tf_op jit(solution)/shard_map/all_to_all | solution.py:126
  26.7 0.9 copy-done.13
  28.0 1.2 %copy.19 = bf16[512,4,128]{2,1,0:T(4,128)(2,1)} copy(bf16[512,4,128]{0,1,2:T(4,128)(2,1)S(1)} %bitcast.57) | data formatting | bytes 1048576 | tf_op jit(solution)/shard_map/transpose | solution.py:115
  29.4 1.2 %copy.17 = bf16[512,128,4]{1,2,0:T(4,128)(2,1)} copy(bf16[512,128,4]{0,2,1:T(4,128)(2,1)S(1)} %reshape.53) | data formatting | bytes 1048576 | tf_op jit(solution)/shard_map/reshape | solution.py:115
  30.6 2.1 %copy_bitcast_fusion.2 = (bf16[512,512]{1,0:T(8,128)(2,1)S(1)}, bf16[512,512]{1,0:T(8,128)(2,1)}) fusion(bf16[64,8,4,128]{3,2,1,0:T(4,128)(2,1)} %bitcast.60, bf16[64,8,4,128]{3,2,1,0:T(4,128)(2,1)} %bitcast.61), kind=kLoop, calls=%fused_computation.2 | loop fusion | bytes 2097152 | tf_op jit(solution)/shard_map/reshape | solution.py:115
  32.8 26.4 %all-to-all-done.in_ref = bf16[128,32,128]{2,1,0:T(8,128)(2,1)S(1)} async-done(((bf16[128,32,128]{2,1,0:T(8,128)(2,1)}), bf16[128,32,128]{2,1,0:T(8,128)(2,1)S(1)}, u32[]{:S(2)}, u32[]{:S(2)}) %all-to-all-start) | async-done | bytes 1048608 | tf_op jit(solution)/shard_map/all_to_all | solution.py:126
  59.1 1.0 copy-done.1
  60.2 2.6 %shard_map.95 = (bf16[128,32,128]{2,1,0:T(8,128)(2,1)S(1)}, f32[4,512,128]{2,1,0:T(8,128)S(1)}) custom-call(bf16[128,32,128]{2,1,0:T(8,128)(2,1)S(1)} %all-to-all-done.in_ref, bf16[512,512]{1,0:T(8,128)(2,1)S(1)} %bitcast.50, bf16[512,512]{1,0:T(8,128)(2,1)S(1)} %copy-done.1, bf16[512,512]{1,0:T(8,128)(2,1)S(1)} %get-tuple-element.11.unmixp_ref, ...), custom_call_target="tpu_custom_call" | custom-call | tf_op jit(solution)/shard_map/pallas_call | solution.py:78
  62.8 1.0 copy-done.6
  63.8 1.0 copy-done.7
  64.7 6.7 %all-to-all-start.1 = ((bf16[128,32,128]{2,1,0:T(8,128)(2,1)}), bf16[128,32,128]{2,1,0:T(8,128)(2,1)S(1)}, u32[]{:S(2)}, u32[]{:S(2)}) async-start(bf16[128,32,128]{2,1,0:T(8,128)(2,1)} %copy-done.6), calls=%async_computation.1 | async-start | bytes 2097152 | tf_op jit(solution)/shard_map/all_to_all | solution.py:138
  71.8 0.7 fusion
  72.5 1.9 %collective-permute-start = (bf16[4,512,2,32]{1,3,2,0:T(8,128)(2,1)}, bf16[4,512,2,32]{1,3,2,0:T(8,128)(2,1)S(1)}, u32[]{:S(2)}, u32[]{:S(2)}) collective-permute-start(bf16[4,512,2,32]{1,3,2,0:T(8,128)(2,1)} %fusion), channel_id=1, source_target_pairs={{0,1},{1,0},{2,3},{3,2},{4,5},{5,4},{6,7},{7,6},{8,9},{9,8},{10,11... | collective-permute-start | bytes 786440 | tf_op jit(solution)/shard_map/ppermute | solution.py:96
  74.8 1.2 %copy.23 = bf16[512,4,128]{2,1,0:T(4,128)(2,1)} copy(bf16[512,4,128]{0,1,2:T(4,128)(2,1)S(1)} %bitcast.56) | data formatting | bytes 1048576 | tf_op jit(solution)/shard_map/transpose | solution.py:115
  76.9 2.6 %collective-permute-start.1 = (bf16[4,512,32]{1,2,0:T(8,128)(2,1)S(1)}, bf16[4,512,32]{1,2,0:T(8,128)(2,1)S(1)}, u32[]{:S(2)}, u32[]{:S(2)}) collective-permute-start(bf16[4,512,32]{1,2,0:T(8,128)(2,1)S(1)} %fusion.2), channel_id=1, source_target_pairs={{0,2},{2,0},{1,3},{3,1},{4,6},{6,4},{5,7},{7,5},{8,10},{10,8},{9,1... | collective-permute-start | bytes 393224 | tf_op jit(solution)/shard_map/ppermute | solution.py:100
  79.7 7.5 %collective-permute-done.1 = bf16[4,512,32]{1,2,0:T(8,128)(2,1)S(1)} collective-permute-done((bf16[4,512,32]{1,2,0:T(8,128)(2,1)S(1)}, bf16[4,512,32]{1,2,0:T(8,128)(2,1)S(1)}, u32[]{:S(2)}, u32[]{:S(2)}) %collective-permute-start.1) | collective-permute-done | bytes 131104 | tf_op jit(solution)/shard_map/ppermute | solution.py:100
  87.2 0.7 fusion.1
  87.9 15.5 %all-to-all-done.1.in_ref = bf16[128,32,128]{2,1,0:T(8,128)(2,1)S(1)} async-done(((bf16[128,32,128]{2,1,0:T(8,128)(2,1)}), bf16[128,32,128]{2,1,0:T(8,128)(2,1)S(1)}, u32[]{:S(2)}, u32[]{:S(2)}) %all-to-all-start.1) | async-done | bytes 1048608 | tf_op jit(solution)/shard_map/all_to_all | solution.py:138
  103.4 2.5 %shard_map.96 = (bf16[2048,128]{1,0:T(8,128)(2,1)}, bf16[2048,128]{1,0:T(8,128)(2,1)}) custom-call(bf16[128,32,128]{2,1,0:T(8,128)(2,1)S(1)} %all-to-all-done.1.in_ref, bf16[512,512]{1,0:T(8,128)(2,1)S(1)} %get-tuple-element.14.unmixt_ref, bf16[512,512]{1,0:T(8,128)(2,1)S(1)} %get-tuple-element.13.mixp_ref), custom_call_target="tpu_custom_call" | custom-call | tf_op jit(solution)/shard_map/pallas_call | solution.py:78
  (33 shorter events, 2.2 us)
Async XLA Ops:
  0.6 1.0 copy-start.2
  1.7 1.0 copy-start.4
  2.7 1.0 copy-start.9
  3.8 1.0 copy-start.10
  6.6 20.0 %copy-start.12 = (bf16[512,4,128]{2,1,0:T(4,128)(2,1)S(1)}, bf16[512,4,128]{2,1,0:T(4,128)(2,1)}, u32[]{:S(2)}) copy-start(bf16[512,4,128]{2,1,0:T(4,128)(2,1)} %param.9) | copy-start | bytes 1572868
  6.6 52.5 %all-to-all-start = ((bf16[128,32,128]{2,1,0:T(8,128)(2,1)}), bf16[128,32,128]{2,1,0:T(8,128)(2,1)S(1)}, u32[]{:S(2)}, u32[]{:S(2)}) async-start(bf16[128,32,128]{2,1,0:T(8,128)(2,1)} %shard_map.94), calls=%async_computation | async-start | bytes 2097152 | tf_op jit(solution)/shard_map/all_to_all | solution.py:126
  26.6 1.0 copy-start.13
  28.0 1.2 %copy-start = (bf16[512,512]{1,0:T(8,128)(2,1)S(1)}, bf16[512,512]{1,0:T(8,128)(2,1)}, u32[]{:S(2)}) copy-start(bf16[512,512]{1,0:T(8,128)(2,1)} %mix_ref.3) | copy-start | bytes 1572868
  59.1 1.0 copy-start.1
  62.8 1.0 copy-start.6
  63.8 1.0 copy-start.7
  64.7 6.7 %copy-start.8 = (f32[4,512,128]{2,1,0:T(8,128)S(1)}, f32[4,512,128]{2,1,0:T(8,128)}, u32[]{:S(2)}) copy-start(f32[4,512,128]{2,1,0:T(8,128)} %copy-done.7) | copy-start | bytes 3145732
  64.7 38.7 %all-to-all-start.1 = ((bf16[128,32,128]{2,1,0:T(8,128)(2,1)}), bf16[128,32,128]{2,1,0:T(8,128)(2,1)S(1)}, u32[]{:S(2)}, u32[]{:S(2)}) async-start(bf16[128,32,128]{2,1,0:T(8,128)(2,1)} %copy-done.6), calls=%async_computation.1 | async-start | bytes 2097152 | tf_op jit(solution)/shard_map/all_to_all | solution.py:138
  71.7 2.7 %copy-start.3 = (bf16[512,512]{1,0:T(8,128)(2,1)S(1)}, bf16[512,512]{1,0:T(8,128)(2,1)}, u32[]{:S(2)}) copy-start(bf16[512,512]{1,0:T(8,128)(2,1)} %mix_ref.2) | copy-start | bytes 1572868
  72.5 4.3 %collective-permute-start = (bf16[4,512,2,32]{1,3,2,0:T(8,128)(2,1)}, bf16[4,512,2,32]{1,3,2,0:T(8,128)(2,1)S(1)}, u32[]{:S(2)}, u32[]{:S(2)}) collective-permute-start(bf16[4,512,2,32]{1,3,2,0:T(8,128)(2,1)} %fusion), channel_id=1, source_target_pairs={{0,1},{1,0},{2,3},{3,2},{4,5},{5,4},{6,7},{7,6},{8,9},{9,8},{10,11... | collective-permute-start | bytes 786440 | tf_op jit(solution)/shard_map/ppermute | solution.py:96
  74.8 1.2 %copy-start.5 = (bf16[512,512]{1,0:T(8,128)(2,1)S(1)}, bf16[512,512]{1,0:T(8,128)(2,1)}, u32[]{:S(2)}) copy-start(bf16[512,512]{1,0:T(8,128)(2,1)} %unmix_ref.1) | copy-start | bytes 1572868
  76.8 2.8 %copy-start.11 = (bf16[512,4,128]{2,1,0:T(4,128)(2,1)S(1)}, bf16[512,4,128]{2,1,0:T(4,128)(2,1)}, u32[]{:S(2)}) copy-start(bf16[512,4,128]{2,1,0:T(4,128)(2,1)} %copy.23) | copy-start | bytes 1572868
  76.9 10.3 %collective-permute-start.1 = (bf16[4,512,32]{1,2,0:T(8,128)(2,1)S(1)}, bf16[4,512,32]{1,2,0:T(8,128)(2,1)S(1)}, u32[]{:S(2)}, u32[]{:S(2)}) collective-permute-start(bf16[4,512,32]{1,2,0:T(8,128)(2,1)S(1)} %fusion.2), channel_id=1, source_target_pairs={{0,2},{2,0},{1,3},{3,1},{4,6},{6,4},{5,7},{7,5},{8,10},{10,8},{9,1... | collective-permute-start | bytes 393224 | tf_op jit(solution)/shard_map/ppermute | solution.py:100

commit v3 on v1

v3 whole, which is shorter than its diff:
```python
import functools

import jax
import jax.numpy as jnp
from jax import lax
from jax.experimental import pallas as pl
from jax.experimental.pallas import tpu as pltpu
from jax.sharding import PartitionSpec as P

SUBLANES = 8
WHOLE_VMEM = 62 * 1024 * 1024
MOST_VMEM = 24 * 1024 * 1024


def dot(left, right, left_dim=1):
    return lax.dot_general(left, right, (((left_dim,), (0,)), ((), ())), preferred_element_type=jnp.float32)


class Copies:
    def __init__(self, sems):
        self.sems, self.started = sems, []

    def start(self, src, dst):
        copy = pltpu.make_async_copy(src, dst, self.sems.at[len(self.started)])
        copy.start()
        self.started.append(copy)
        return copy


def scatter_rows(slab, product, stage, out_buf, part):
    block, width = product.shape
    channels = width // slab
    for g in range(slab):
        stage[pl.ds(g, block, stride=slab), :] = product[:, g * channels : (g + 1) * channels]
    rows = slab * slab
    out_buf[:, part * rows : (part + 1) * rows, :] = (
        stage[...].astype(jnp.bfloat16).reshape(block // slab, rows, channels)
    )


def gather_rows(slab, in_ref, part):
    groups, _, channels = in_ref.shape
    rows = slab * slab
    tiles = rows // SUBLANES
    got = in_ref[:, part * rows : (part + 1) * rows, :].astype(jnp.float32)
    got = got.reshape(groups // 2, 2, tiles, SUBLANES, channels)
    turned = pltpu.roll(got.reshape(groups * tiles, SUBLANES, channels), slab, axis=1).reshape(got.shape)
    low = lax.broadcasted_iota(jnp.int32, (groups // 2, tiles, SUBLANES, channels), 2) < slab
    even = jnp.where(low, got[:, 0], turned[:, 1]).astype(jnp.bfloat16)
    odd = jnp.where(low, turned[:, 0], got[:, 1]).astype(jnp.bfloat16)
    lanes = [half[:, t].reshape(groups * slab, channels) for t in range(tiles) for half in (even, odd)]
    return jnp.concatenate(lanes, axis=1)


def lanes_of(ref, slab):
    block = ref.shape[0] // slab
    return jnp.concatenate([ref[a * block : (a + 1) * block, :] for a in range(slab)], axis=1)


def part_of(ref, rows, part):
    return ref.at[:, pl.ds(part * rows, rows)]


def far_of(weights, shape):
    block, channels = weights[0].shape[0], shape[2]
    rows = [weight.reshape(block, block // channels, channels).transpose(1, 0, 2) for weight in weights]
    return jnp.concatenate(rows, axis=0).reshape(shape)


def near_of(far, block):
    parts = block // far.shape[2]
    step = far.shape[0] // parts
    return jnp.concatenate([far[t * step : (t + 1) * step].reshape(block, far.shape[2]) for t in range(parts)], axis=1)


def before_kernel(slab, tok_hbm, cot_hbm, mix_hbm, unmix_hbm, out_ref, tok, cot, mix, unmix, stage, out_buf, sems):
    copies = Copies(sems)
    got = [copies.start(src, dst) for src, dst in ((mix_hbm, mix), (tok_hbm, tok), (unmix_hbm, unmix), (cot_hbm, cot))]
    rows = slab * slab
    given = []
    for part, (weight, data, left_dim) in enumerate(((mix, tok, 0), (unmix, cot, 1))):
        got[2 * part].wait()
        got[2 * part + 1].wait()
        scatter_rows(slab, dot(weight[...], lanes_of(data, slab), left_dim), stage.at[part], out_buf, part)
        given.append(copies.start(part_of(out_buf, rows, part), part_of(out_ref, rows, part)))
    for copy in given:
        copy.wait()


def between_kernel(
    slab, in_hbm, ker_hbm, far_hbm, out_ref, term_ref, in_ref, ker, mix_rows, unmix_rows, stage, out_buf, term_buf, sems
):
    channels = in_ref.shape[2]
    block = ker.shape[1]
    rows = slab * slab
    copies = Copies(sems)
    got_in = copies.start(in_hbm, in_ref)
    half = mix_rows.shape[0]
    got_mix = copies.start(far_hbm.at[pl.ds(0, half)], mix_rows)
    got_unmix = copies.start(far_hbm.at[pl.ds(half, half)], unmix_rows)
    got_ker = copies.start(ker_hbm, ker)
    got_in.wait()
    mixed = gather_rows(slab, in_ref, 0)
    cotangent = gather_rows(slab, in_ref, 1)
    got_mix.wait()
    mix = near_of(mix_rows, block)
    spectrum = dot(mix, mixed, 0).astype(jnp.bfloat16).astype(jnp.float32)
    got_unmix.wait()
    unmix = near_of(unmix_rows, block)
    gradf = dot(unmix, cotangent).astype(jnp.bfloat16).astype(jnp.float32)
    terms = spectrum * gradf
    got_ker.wait()
    for i in range(slab):
        term_buf[i] = terms[:, i * channels : (i + 1) * channels]
    given = [copies.start(term_buf, term_ref)]
    weight = jnp.concatenate([ker[i] for i in range(slab)], axis=1)
    filtered = (weight * spectrum).astype(jnp.bfloat16)
    scatter_rows(slab, dot(unmix, filtered, 0), stage.at[0], out_buf, 0)
    given.append(copies.start(part_of(out_buf, rows, 0), part_of(out_ref, rows, 0)))
    grad_spectrum = (weight * gradf).astype(jnp.bfloat16)
    scatter_rows(slab, dot(mix, grad_spectrum), stage.at[1], out_buf, 1)
    given.append(copies.start(part_of(out_buf, rows, 1), part_of(out_ref, rows, 1)))
    for copy in given:
        copy.wait()


def after_kernel(slab, in_hbm, unmix_hbm, mix_hbm, res_ref, tok_ref, in_ref, unmix, mix, out_buf, sems):
    channels = in_ref.shape[2]
    block = unmix.shape[0]
    copies = Copies(sems)
    got_in = copies.start(in_hbm, in_ref)
    got = [copies.start(unmix_hbm, unmix), copies.start(mix_hbm, mix)]
    got_in.wait()
    arrived = [gather_rows(slab, in_ref, part) for part in range(2)]
    given = []
    for part, (weight, left_dim, out_ref) in enumerate(((unmix, 0, res_ref), (mix, 1, tok_ref))):
        got[part].wait()
        product = dot(weight[...], arrived[part], left_dim).astype(jnp.bfloat16)
        for i in range(slab):
            out_buf[part, i * block : (i + 1) * block, :] = product[:, i * channels : (i + 1) * channels]
        given.append(copies.start(out_buf.at[part], out_ref))
    for copy in given:
        copy.wait()


def call(kernel, outs, specs, scratch, copies, limit, flops, aliases, *args):
    return pl.pallas_call(
        kernel,
        out_shape=outs,
        in_specs=[pl.BlockSpec(memory_space=space) for space in specs],
        out_specs=jax.tree.map(lambda _: pl.BlockSpec(memory_space=pl.ANY), outs),
        scratch_shapes=[*scratch, pltpu.SemaphoreType.DMA((copies,))],
        input_output_aliases=aliases,
        compiler_params=pltpu.CompilerParams(vmem_limit_bytes=limit),
        cost_estimate=pl.CostEstimate(flops=flops, bytes_accessed=4 * 1024 * 1024, transcendentals=0),
    )(*args)


def kernels(block, slab, channels):
    local_len, groups = block * slab, block // slab
    bf16, f32 = jnp.bfloat16, jnp.float32
    ANY, VMEM = pl.ANY, pltpu.VMEM
    message = jax.ShapeDtypeStruct((groups, 2 * slab * slab, channels), bf16)
    flat = jax.ShapeDtypeStruct((local_len, channels), bf16)
    stage = VMEM((2, local_len, channels), f32)
    buffer = VMEM(message.shape, bf16)
    piece, matrix = VMEM((local_len, channels), bf16), VMEM((block, block), bf16)
    flops = 2 * block * block * slab * channels
    before = functools.partial(
        call, functools.partial(before_kernel, slab), message, [ANY] * 4,
        [piece, piece, matrix, matrix, stage, buffer], 6, WHOLE_VMEM, 2 * flops, {},
    )
    between = functools.partial(
        call, functools.partial(between_kernel, slab), (message, jax.ShapeDtypeStruct((slab, block, channels), f32)),
        [ANY] * 3,
        [buffer, VMEM((slab, block, channels), f32)] + [VMEM((groups // 2, 2 * slab * slab, channels), bf16)] * 2
        + [stage, buffer, VMEM((slab, block, channels), f32)], 7, MOST_VMEM, 4 * flops, {1: 1, 2: 0},
    )
    after = functools.partial(
        call, functools.partial(after_kernel, slab), (flat, flat), [ANY] * 3,
        [buffer, matrix, matrix, VMEM((2, local_len, channels), bf16)], 5, MOST_VMEM, 2 * flops, {},
    )
    return before, between, after


def batch_sum(terms):
    inner, outer, channels = terms.shape
    quarter = channels // 4
    place = lax.axis_index("batch")
    core, side = lax.rem(place, 2), lax.div(place, 2)
    parts = terms.reshape(inner, outer, 2, 2, quarter)
    mine = lax.dynamic_index_in_dim(parts, core, 3, keepdims=False)
    other = lax.dynamic_index_in_dim(parts, 1 - core, 3, keepdims=False).astype(jnp.bfloat16)
    got = lax.ppermute(other, "batch", [(0, 1), (1, 0), (2, 3), (3, 2)])
    pair = mine + got.astype(jnp.float32)
    keep = lax.dynamic_index_in_dim(pair, side, 2, keepdims=False)
    give = lax.dynamic_index_in_dim(pair, 1 - side, 2, keepdims=False).astype(jnp.bfloat16)
    got = lax.ppermute(give, "batch", [(0, 2), (2, 0), (1, 3), (3, 1)])
    return (keep + got.astype(jnp.float32)).transpose(1, 0, 2)


def body(tokens, grad_out, kernel, mix_inner, mix_outer, unmix_outer, unmix_inner):
    local_len, channels = tokens.shape[1:]
    block = mix_inner.shape[0]
    slab = local_len // block
    before, between, after = kernels(block, slab, channels)
    sent = before(tokens.reshape(local_len, channels), grad_out.reshape(local_len, channels), mix_inner, unmix_inner)
    here = lax.all_to_all(sent, "seq", split_axis=0, concat_axis=0, tiled=True)
    far = far_of((mix_outer, unmix_outer), (block // slab, 2 * slab * slab, channels))
    sent, terms = between(here, kernel.transpose(1, 0, 2).astype(jnp.float32), far)
    back = lax.all_to_all(sent, "seq", split_axis=0, concat_axis=0, tiled=True)
    grad_kernel = batch_sum(terms)
    output, grad_tokens = after(back, unmix_inner, mix_inner)
    return (output.reshape(1, local_len, channels), grad_tokens.reshape(1, local_len, channels), grad_kernel)


def solution(mesh):
    return jax.shard_map(
        body,
        mesh=mesh,
        in_specs=(
            P("batch", "seq", None),
            P("batch", "seq", None),
            P(None, "seq", None),
            P(),
            P(),
            P(),
            P(),
        ),
        out_specs=(P("batch", "seq", None), P("batch", "seq", None), P(None, "seq", "batch")),
        check_vma=False,
    )
```

time: 114 us -> 102 us (0.89)
  local copies, waits for them, and re-layouts: 19.6 us -> 2.72 us
  Pallas kernels: 0 us -> 9.38 us
  matrix products: 8.71 us -> 0 us
  waiting for transfers between devices: 51.5 us -> 54.1 us
  other arithmetic: 1.01 us -> 3.05 us
    pallas_call x0 -> x3, Pallas kernels: none -> 9.38 us  [call(): pl.pallas_call(kernel, out_shape=outs, in_specs=[pl.BlockSpec(memory_spac...]
    dot_general x8 -> x0, matrix products: 8.71 us -> none  [product(): jnp.einsum(pattern, left, right, preferred_element_type=jnp.float32)]
    convert_element_type x6 -> x0, local copies, waits for them, and re-layouts: 5.23 us -> none  [product(): jnp.einsum(pattern, left, right, preferred_element_type=jnp.float32)]
    unnamed x35 -> x10, local copies, waits for them, and re-layouts: 4.86 us -> 0.09 us
    reshape x6 -> x0, local copies, waits for them, and re-layouts: 4.46 us -> none  [the longest x2 1.32 us: body(): mix_inner.reshape(block_len, groups, slab)]
    ppermute x1, waiting for transfers between devices: 4.53 us -> 7.25 us  [batch_sum(): got = lax.ppermute(give, 'batch', [(0, 2), (2, 0), (1, 3), (3, 1)])]
    another operation x2 -> x0, local copies, waits for them, and re-layouts: 2.33 us -> none  [the longest x1 1.18 us: body(): jnp.stack([inner_mixed.reshape(groups, slab * slab, channels), grad_inner...]
    all_to_all x1, waiting for transfers between devices: 29 us -> 31.1 us  [body(): here = lax.all_to_all(sent, 'seq', split_axis=0, concat_axis=0, tiled=True)]
where the time goes in v3:
time: 102 us; the launch traced here: 101 us
  waiting for transfers between devices  54.1 us (53%)
  starting transfers between devices  31.1 us (30%)
  Pallas kernels  9.38 us (9%)
  other arithmetic  3.05 us (3%)
  local copies, waits for them, and re-layouts  2.72 us (3%)
    all_to_all x1, waiting for transfers between devices, body(): here = lax.all_to_all(sent, 'seq', split_axis=0, concat_axis=0, tiled=True)  31.1 us
    all_to_all x1, starting transfers between devices, body(): here = lax.all_to_all(sent, 'seq', split_axis=0, concat_axis=0, tiled=True)  20 us
    all_to_all x1, waiting for transfers between devices, body(): back = lax.all_to_all(sent, 'seq', split_axis=0, concat_axis=0, tiled=True)  14.3 us
    pallas_call x3, Pallas kernels, call(): pl.pallas_call(kernel, out_shape=outs, in_specs=[pl.BlockSpec(memory_spac...  9.38 us
    ppermute x1, waiting for transfers between devices, batch_sum(): got = lax.ppermute(give, 'batch', [(0, 2), (2, 0), (1, 3), (3, 1)])  7.25 us
    all_to_all x1, starting transfers between devices, body(): back = lax.all_to_all(sent, 'seq', split_axis=0, concat_axis=0, tiled=True)  6.54 us
    ppermute x1, starting transfers between devices, batch_sum(): got = lax.ppermute(give, 'batch', [(0, 2), (2, 0), (1, 3), (3, 1)])  2.64 us
  transfers between devices with their start and end apart: 4, of which 4 were waited for; matrix products, arithmetic and copies ran while one was open for 6% of the time, Pallas kernels for 0%

profile of v3, /device:TPU:8, one launch (start us, length us, event | category | flops | bytes accessed | tf_op | source)
XLA Modules:
  0.0 101.1 jit_solution(13575526448191046804)
XLA Ops:
  0.6 0.0 copy-start
  0.6 3.2 %shard_map.94 = bf16[128,32,128]{2,1,0:T(8,128)(2,1)} custom-call(bf16[2048,128]{1,0:T(8,128)(2,1)} %bitcast.36, bf16[2048,128]{1,0:T(8,128)(2,1)} %bitcast.37, bf16[512,512]{1,0:T(8,128)(2,1)} %mix_hbm.3, bf16[512,512]{1,0:T(8,128)(2,1)} %unmix_hbm.3), custom_call_target="tpu_custom_call" | custom-call | flops 536870912 | bytes 4194304 | tf_op jit(solution)/shard_map/pallas_call | solution.py:147
  3.8 0.0 copy-start.4
  3.8 20.0 %all-to-all-start = ((bf16[128,32,128]{2,1,0:T(8,128)(2,1)}), bf16[128,32,128]{2,1,0:T(8,128)(2,1)S(1)}, u32[]{:S(2)}, u32[]{:S(2)}) async-start(bf16[128,32,128]{2,1,0:T(8,128)(2,1)} %shard_map.94), calls=%async_computation | async-start | bytes 2097152 | tf_op jit(solution)/shard_map/all_to_all | solution.py:208
  23.8 0.0 copy-done
  23.8 0.2 bitcast_bitcast_fusion
  24.0 0.0 copy-start.3
  24.0 1.1 %pad_maximum_fusion = bf16[8,512,128]{2,1,0:T(8,128)(2,1)} fusion(bf16[4,512,128]{2,1,0:T(8,128)(2,1)S(1)} %get-tuple-element.11, bf16[4,512,128]{2,1,0:T(8,128)(2,1)S(1)} %get-tuple-element.12), kind=kLoop, calls=%fused_computation | loop fusion | flops 524288 | bytes 2097152 | tf_op jit(solution)/shard_map/concatenate | solution.py:67
  25.1 0.1 copy-done.3
  25.2 0.1 convert_bitcast_fusion.ker_hbm
  25.2 31.1 %all-to-all-done.in_hbm = bf16[128,32,128]{2,1,0:T(8,128)(2,1)S(1)} async-done(((bf16[128,32,128]{2,1,0:T(8,128)(2,1)}), bf16[128,32,128]{2,1,0:T(8,128)(2,1)S(1)}, u32[]{:S(2)}, u32[]{:S(2)}) %all-to-all-start) | async-done | bytes 1048608 | tf_op jit(solution)/shard_map/all_to_all | solution.py:208
  56.3 4.0 %shard_map.95 = (bf16[128,32,128]{2,1,0:T(8,128)(2,1)}, f32[4,512,128]{2,1,0:T(8,128)S(1)}) custom-call(bf16[128,32,128]{2,1,0:T(8,128)(2,1)S(1)} %all-to-all-done.in_hbm, f32[4,512,128]{2,1,0:T(8,128)S(1)} %convert_bitcast_fusion.ker_hbm, bf16[128,32,128]{2,1,0:T(8,128)(2,1)} %bitcast.5.far_hbm), custom_call_target="tpu_custom_call", output_to_operand_aliasing={{1}: (1, {}), {0}: (2, {})} | custom-call | flops 1073741824 | bytes 4194304 | tf_op jit(solution)/shard_map/pallas_call | solution.py:147
  60.3 6.5 %all-to-all-start.1 = ((bf16[128,32,128]{2,1,0:T(8,128)(2,1)}), bf16[128,32,128]{2,1,0:T(8,128)(2,1)S(1)}, u32[]{:S(2)}, u32[]{:S(2)}) async-start(bf16[128,32,128]{2,1,0:T(8,128)(2,1)} %get-tuple-element.7), calls=%async_computation.1 | async-start | bytes 2097152 | tf_op jit(solution)/shard_map/all_to_all | solution.py:211
  66.9 1.3 %copy.20 = f32[4,512,128]{1,2,0:T(8,128)} copy(f32[4,512,128]{2,1,0:T(8,128)S(1)} %get-tuple-element.10) | data formatting | bytes 2097152 | tf_op jit(solution)/shard_map/pallas_call | solution.py:147
  68.2 1.1 %fusion = bf16[4,512,2,32]{1,3,2,0:T(8,128)(2,1)S(1)} fusion(f32[4,512,2,2,32]{1,4,3,2,0:T(8,128)} %bitcast.34, s32[]{:T(128)S(6)} %select_n.15), kind=kLoop, calls=%fused_computation.6 | loop fusion | bytes 524292 | tf_op jit(solution)/shard_map/convert_element_type | solution.py:193
  69.3 1.9 %collective-permute-start = (bf16[4,512,2,32]{1,3,2,0:T(8,128)(2,1)S(1)}, bf16[4,512,2,32]{1,3,2,0:T(8,128)(2,1)S(1)}, u32[]{:S(2)}, u32[]{:S(2)}) collective-permute-start(bf16[4,512,2,32]{1,3,2,0:T(8,128)(2,1)S(1)} %fusion), channel_id=1, source_target_pairs={{0,1},{1,0},{2,3},{3,2},{4,5},{5,4},{6,7},{7,6},{8,9},{9,8},{10,11... | collective-permute-start | bytes 786440 | tf_op jit(solution)/shard_map/ppermute | solution.py:194
  71.2 1.5 %collective-permute-done = bf16[4,512,2,32]{1,3,2,0:T(8,128)(2,1)S(1)} collective-permute-done((bf16[4,512,2,32]{1,3,2,0:T(8,128)(2,1)S(1)}, bf16[4,512,2,32]{1,3,2,0:T(8,128)(2,1)S(1)}, u32[]{:S(2)}, u32[]{:S(2)}) %collective-permute-start) | collective-permute-done | bytes 262176 | tf_op jit(solution)/shard_map/ppermute | solution.py:194
  72.7 1.2 %bitcast_add_fusion = f32[4,512,2,32]{1,3,2,0:T(8,128)S(1)} fusion(bf16[4,512,2,32]{1,3,2,0:T(8,128)(2,1)S(1)} %collective-permute-done, f32[4,512,2,2,32]{1,4,3,2,0:T(8,128)} %bitcast.35, s32[]{:T(128)S(6)} %select_n.14), kind=kLoop, calls=%fused_computation.4 | loop fusion | flops 262144 | bytes 1310724 | tf_op jit(solution)/shard_map/add | solution.py:195
  73.9 0.0 copy-start.1
  73.9 2.6 %collective-permute-start.1 = (bf16[4,512,32]{1,2,0:T(8,128)(2,1)S(1)}, bf16[4,512,32]{1,2,0:T(8,128)(2,1)S(1)}, u32[]{:S(2)}, u32[]{:S(2)}) collective-permute-start(bf16[4,512,32]{1,2,0:T(8,128)(2,1)S(1)} %fusion.2), channel_id=1, source_target_pairs={{0,2},{2,0},{1,3},{3,1},{4,6},{6,4},{5,7},{7,5},{8,10},{10,8},{9,1... | collective-permute-start | bytes 393224 | tf_op jit(solution)/shard_map/ppermute | solution.py:198
  76.6 7.2 %collective-permute-done.1 = bf16[4,512,32]{1,2,0:T(8,128)(2,1)S(1)} collective-permute-done((bf16[4,512,32]{1,2,0:T(8,128)(2,1)S(1)}, bf16[4,512,32]{1,2,0:T(8,128)(2,1)S(1)}, u32[]{:S(2)}, u32[]{:S(2)}) %collective-permute-start.1) | collective-permute-done | bytes 131104 | tf_op jit(solution)/shard_map/ppermute | solution.py:198
  83.8 0.7 fusion.1
  84.6 14.3 %all-to-all-done.1.in_hbm = bf16[128,32,128]{2,1,0:T(8,128)(2,1)S(1)} async-done(((bf16[128,32,128]{2,1,0:T(8,128)(2,1)}), bf16[128,32,128]{2,1,0:T(8,128)(2,1)S(1)}, u32[]{:S(2)}, u32[]{:S(2)}) %all-to-all-start.1) | async-done | bytes 1048608 | tf_op jit(solution)/shard_map/all_to_all | solution.py:211
  98.9 2.2 %shard_map.96 = (bf16[2048,128]{1,0:T(8,128)(2,1)}, bf16[2048,128]{1,0:T(8,128)(2,1)}) custom-call(bf16[128,32,128]{2,1,0:T(8,128)(2,1)S(1)} %all-to-all-done.1.in_hbm, bf16[512,512]{1,0:T(8,128)(2,1)S(1)} %copy-done.2, bf16[512,512]{1,0:T(8,128)(2,1)S(1)} %copy-done.1), custom_call_target="tpu_custom_call" | custom-call | flops 536870912 | bytes 4194304 | tf_op jit(solution)/shard_map/pallas_call | solution.py:147
  (5 shorter events, 0.0 us)
Async XLA Ops:
  0.6 23.2 %copy-start = (bf16[512,512]{1,0:T(8,128)(2,1)S(1)}, bf16[512,512]{1,0:T(8,128)(2,1)}, u32[]{:S(2)}) copy-start(bf16[512,512]{1,0:T(8,128)(2,1)} %param.11) | copy-start | bytes 1572868
  3.8 20.0 %copy-start.4 = (bf16[512,512]{1,0:T(8,128)(2,1)S(1)}, bf16[512,512]{1,0:T(8,128)(2,1)}, u32[]{:S(2)}) copy-start(bf16[512,512]{1,0:T(8,128)(2,1)} %param.12) | copy-start | bytes 1572868
  3.8 52.5 %all-to-all-start = ((bf16[128,32,128]{2,1,0:T(8,128)(2,1)}), bf16[128,32,128]{2,1,0:T(8,128)(2,1)S(1)}, u32[]{:S(2)}, u32[]{:S(2)}) async-start(bf16[128,32,128]{2,1,0:T(8,128)(2,1)} %shard_map.94), calls=%async_computation | async-start | bytes 2097152 | tf_op jit(solution)/shard_map/all_to_all | solution.py:208
  24.0 1.1 %copy-start.3 = (bf16[512,4,128]{2,1,0:T(4,128)(2,1)S(1)}, bf16[512,4,128]{2,1,0:T(4,128)(2,1)}, u32[]{:S(2)}) copy-start(bf16[512,4,128]{2,1,0:T(4,128)(2,1)} %param.9) | copy-start | bytes 1572868
  60.3 38.6 %all-to-all-start.1 = ((bf16[128,32,128]{2,1,0:T(8,128)(2,1)}), bf16[128,32,128]{2,1,0:T(8,128)(2,1)S(1)}, u32[]{:S(2)}, u32[]{:S(2)}) async-start(bf16[128,32,128]{2,1,0:T(8,128)(2,1)} %get-tuple-element.7), calls=%async_computation.1 | async-start | bytes 2097152 | tf_op jit(solution)/shard_map/all_to_all | solution.py:211
  69.3 3.4 %collective-permute-start = (bf16[4,512,2,32]{1,3,2,0:T(8,128)(2,1)S(1)}, bf16[4,512,2,32]{1,3,2,0:T(8,128)(2,1)S(1)}, u32[]{:S(2)}, u32[]{:S(2)}) collective-permute-start(bf16[4,512,2,32]{1,3,2,0:T(8,128)(2,1)S(1)} %fusion), channel_id=1, source_target_pairs={{0,1},{1,0},{2,3},{3,2},{4,5},{5,4},{6,7},{7,6},{8,9},{9,8},{10,11... | collective-permute-start | bytes 786440 | tf_op jit(solution)/shard_map/ppermute | solution.py:194
  72.7 26.2 %copy-start.2 = (bf16[512,512]{1,0:T(8,128)(2,1)S(1)}, bf16[512,512]{1,0:T(8,128)(2,1)}, u32[]{:S(2)}) copy-start(bf16[512,512]{1,0:T(8,128)(2,1)} %unmix_hbm.3) | copy-start | bytes 1572868
  73.9 25.0 %copy-start.1 = (bf16[512,512]{1,0:T(8,128)(2,1)S(1)}, bf16[512,512]{1,0:T(8,128)(2,1)}, u32[]{:S(2)}) copy-start(bf16[512,512]{1,0:T(8,128)(2,1)} %mix_hbm.3) | copy-start | bytes 1572868
  73.9 9.9 %collective-permute-start.1 = (bf16[4,512,32]{1,2,0:T(8,128)(2,1)S(1)}, bf16[4,512,32]{1,2,0:T(8,128)(2,1)S(1)}, u32[]{:S(2)}, u32[]{:S(2)}) collective-permute-start(bf16[4,512,32]{1,2,0:T(8,128)(2,1)S(1)} %fusion.2), channel_id=1, source_target_pairs={{0,2},{2,0},{1,3},{3,1},{4,6},{6,4},{5,7},{7,5},{8,10},{10,8},{9,1... | collective-permute-start | bytes 393224 | tf_op jit(solution)/shard_map/ppermute | solution.py:198

commit v4 on v3

--- a/solution.py
+++ b/solution.py
@@ -61,10 +61,9 @@
     return ref.at[:, pl.ds(part * rows, rows)]
 
 
-def far_of(weights, shape):
-    block, channels = weights[0].shape[0], shape[2]
-    rows = [weight.reshape(block, block // channels, channels).transpose(1, 0, 2) for weight in weights]
-    return jnp.concatenate(rows, axis=0).reshape(shape)
+def far_of(kernel, shape):
+    rows = kernel.transpose(1, 0, 2).reshape(-1, shape[1], shape[2])
+    return jnp.concatenate([rows] * (shape[0] // rows.shape[0]), axis=0)
 
 
 def near_of(far, block):
@@ -87,55 +86,36 @@
         copy.wait()
 
 
-def between_kernel(
-    slab, in_hbm, ker_hbm, far_hbm, out_ref, term_ref, in_ref, ker, mix_rows, unmix_rows, stage, out_buf, term_buf, sems
-):
-    channels = in_ref.shape[2]
-    block = ker.shape[1]
+def between_kernel(slab, in_ref, mix, unmix, far_hbm, out_ref, term_ref, ker_rows, stage, out_buf, term_buf, sems):
+    block, channels = mix.shape[0], in_ref.shape[2]
     rows = slab * slab
     copies = Copies(sems)
-    got_in = copies.start(in_hbm, in_ref)
-    half = mix_rows.shape[0]
-    got_mix = copies.start(far_hbm.at[pl.ds(0, half)], mix_rows)
-    got_unmix = copies.start(far_hbm.at[pl.ds(half, half)], unmix_rows)
-    got_ker = copies.start(ker_hbm, ker)
-    got_in.wait()
-    mixed = gather_rows(slab, in_ref, 0)
-    cotangent = gather_rows(slab, in_ref, 1)
-    got_mix.wait()
-    mix = near_of(mix_rows, block)
-    spectrum = dot(mix, mixed, 0).astype(jnp.bfloat16).astype(jnp.float32)
-    got_unmix.wait()
-    unmix = near_of(unmix_rows, block)
-    gradf = dot(unmix, cotangent).astype(jnp.bfloat16).astype(jnp.float32)
+    got_ker = copies.start(far_hbm.at[pl.ds(0, ker_rows.shape[0])], ker_rows)
+    spectrum = dot(mix[...], gather_rows(slab, in_ref, 0), 0).astype(jnp.bfloat16).astype(jnp.float32)
+    gradf = dot(unmix[...], gather_rows(slab, in_ref, 1)).astype(jnp.bfloat16).astype(jnp.float32)
     terms = spectrum * gradf
-    got_ker.wait()
     for i in range(slab):
         term_buf[i] = terms[:, i * channels : (i + 1) * channels]
+    got_ker.wait()
     given = [copies.start(term_buf, term_ref)]
-    weight = jnp.concatenate([ker[i] for i in range(slab)], axis=1)
+    weight = near_of(ker_rows, block).astype(jnp.float32)
     filtered = (weight * spectrum).astype(jnp.bfloat16)
-    scatter_rows(slab, dot(unmix, filtered, 0), stage.at[0], out_buf, 0)
+    scatter_rows(slab, dot(unmix[...], filtered, 0), stage.at[0], out_buf, 0)
     given.append(copies.start(part_of(out_buf, rows, 0), part_of(out_ref, rows, 0)))
     grad_spectrum = (weight * gradf).astype(jnp.bfloat16)
-    scatter_rows(slab, dot(mix, grad_spectrum), stage.at[1], out_buf, 1)
+    scatter_rows(slab, dot(mix[...], grad_spectrum), stage.at[1], out_buf, 1)
     given.append(copies.start(part_of(out_buf, rows, 1), part_of(out_ref, rows, 1)))
     for copy in given:
         copy.wait()
 
 
-def after_kernel(slab, in_hbm, unmix_hbm, mix_hbm, res_ref, tok_ref, in_ref, unmix, mix, out_buf, sems):
+def after_kernel(slab, in_ref, unmix, mix, res_ref, tok_ref, out_buf, sems):
     channels = in_ref.shape[2]
     block = unmix.shape[0]
     copies = Copies(sems)
-    got_in = copies.start(in_hbm, in_ref)
-    got = [copies.start(unmix_hbm, unmix), copies.start(mix_hbm, mix)]
-    got_in.wait()
-    arrived = [gather_rows(slab, in_ref, part) for part in range(2)]
     given = []
     for part, (weight, left_dim, out_ref) in enumerate(((unmix, 0, res_ref), (mix, 1, tok_ref))):
-        got[part].wait()
-        product = dot(weight[...], arrived[part], left_dim).astype(jnp.bfloat16)
+        product = dot(weight[...], gather_rows(slab, in_ref, part), left_dim).astype(jnp.bfloat16)
         for i in range(slab):
             out_buf[part, i * block : (i + 1) * block, :] = product[:, i * channels : (i + 1) * channels]
         given.append(copies.start(out_buf.at[part], out_ref))
@@ -172,13 +152,13 @@
     )
     between = functools.partial(
         call, functools.partial(between_kernel, slab), (message, jax.ShapeDtypeStruct((slab, block, channels), f32)),
-        [ANY] * 3,
-        [buffer, VMEM((slab, block, channels), f32)] + [VMEM((groups // 2, 2 * slab * slab, channels), bf16)] * 2
-        + [stage, buffer, VMEM((slab, block, channels), f32)], 7, MOST_VMEM, 4 * flops, {1: 1, 2: 0},
+        [VMEM, VMEM, VMEM, ANY],
+        [VMEM((groups // 2, *message.shape[1:]), bf16), stage, buffer, VMEM((slab, block, channels), f32)],
+        4, MOST_VMEM, 4 * flops, {3: 0},
     )
     after = functools.partial(
-        call, functools.partial(after_kernel, slab), (flat, flat), [ANY] * 3,
-        [buffer, matrix, matrix, VMEM((2, local_len, channels), bf16)], 5, MOST_VMEM, 2 * flops, {},
+        call, functools.partial(after_kernel, slab), (flat, flat), [VMEM] * 3,
+        [VMEM((2, local_len, channels), bf16)], 2, MOST_VMEM, 2 * flops, {},
     )
     return before, between, after
 
@@ -206,8 +186,8 @@
     before, between, after = kernels(block, slab, channels)
     sent = before(tokens.reshape(local_len, channels), grad_out.reshape(local_len, channels), mix_inner, unmix_inner)
     here = lax.all_to_all(sent, "seq", split_axis=0, concat_axis=0, tiled=True)
-    far = far_of((mix_outer, unmix_outer), (block // slab, 2 * slab * slab, channels))
-    sent, terms = between(here, kernel.transpose(1, 0, 2).astype(jnp.float32), far)
+    far = far_of(kernel, (block // slab, 2 * slab * slab, channels))
+    sent, terms = between(here, mix_outer, unmix_outer, far)
     back = lax.all_to_all(sent, "seq", split_axis=0, concat_axis=0, tiled=True)
     grad_kernel = batch_sum(terms)
     output, grad_tokens = after(back, unmix_inner, mix_inner)

time: 102 us -> 99.7 us (0.977)
  Pallas kernels: 9.38 us -> 7.54 us
  waiting for transfers between devices: 54.1 us -> 55.8 us
  local copies, waits for them, and re-layouts: 2.72 us -> 1.28 us
    all_to_all x1, waiting for transfers between devices: 14.3 us -> 16.2 us  [body(): back = lax.all_to_all(sent, 'seq', split_axis=0, concat_axis=0, tiled=True)]
    pallas_call x3, Pallas kernels: 9.38 us -> 7.54 us  [call(): pl.pallas_call(kernel, out_shape=outs, in_specs=[pl.BlockSpec(memory_spac...]
    add x1, other arithmetic: 1.18 us -> 0.07 us  [batch_sum(): pair = mine + got.astype(jnp.float32)]
    convert_element_type x1, local copies, waits for them, and re-layouts: 1.07 us -> 0.04 us  [batch_sum(): lax.dynamic_index_in_dim(parts, 1 - core, 3, keepdims=False)]
  transfers between devices with their start and end apart: 4 -> 4, of which waited for: 4 -> 4; matrix products, arithmetic and copies ran while one was open for 6% -> 3% of each run, Pallas kernels for 0% -> 0%
where the time goes in v4:
time: 99.7 us; the launch traced here: 99.3 us
  waiting for transfers between devices  55.8 us (56%)
  starting transfers between devices  31.1 us (31%)
  Pallas kernels  7.54 us (8%)
  other arithmetic  2.82 us (3%)
  local copies, waits for them, and re-layouts  1.28 us (1%)
    all_to_all x1, waiting for transfers between devices, body(): here = lax.all_to_all(sent, 'seq', split_axis=0, concat_axis=0, tiled=True)  31.3 us
    all_to_all x1, starting transfers between devices, body(): here = lax.all_to_all(sent, 'seq', split_axis=0, concat_axis=0, tiled=True)  20 us
    all_to_all x1, waiting for transfers between devices, body(): back = lax.all_to_all(sent, 'seq', split_axis=0, concat_axis=0, tiled=True)  16.2 us
    pallas_call x3, Pallas kernels, call(): pl.pallas_call(kernel, out_shape=outs, in_specs=[pl.BlockSpec(memory_spac...  7.54 us
    ppermute x1, waiting for transfers between devices, batch_sum(): got = lax.ppermute(give, 'batch', [(0, 2), (2, 0), (1, 3), (3, 1)])  6.71 us
    all_to_all x1, starting transfers between devices, body(): back = lax.all_to_all(sent, 'seq', split_axis=0, concat_axis=0, tiled=True)  6.54 us
    ppermute x1, starting transfers between devices, batch_sum(): got = lax.ppermute(give, 'batch', [(0, 2), (2, 0), (1, 3), (3, 1)])  2.63 us
  transfers between devices with their start and end apart: 4, of which 4 were waited for; matrix products, arithmetic and copies ran while one was open for 3% of the time, Pallas kernels for 0%

profile of v4, /device:TPU:8, one launch (start us, length us, event | category | flops | bytes accessed | tf_op | source)
XLA Modules:
  0.0 99.3 jit_solution(11026938375154125785)
XLA Ops:
  0.6 3.1 %shard_map.94 = bf16[128,32,128]{2,1,0:T(8,128)(2,1)} custom-call(bf16[2048,128]{1,0:T(8,128)(2,1)} %bitcast.23, bf16[2048,128]{1,0:T(8,128)(2,1)} %bitcast.24, bf16[512,512]{1,0:T(8,128)(2,1)} %mix.3, bf16[512,512]{1,0:T(8,128)(2,1)} %unmix.3), custom_call_target="tpu_custom_call" | custom-call | flops 536870912 | bytes 4194304 | tf_op jit(solution)/shard_map/pallas_call | solution.py:127
  3.7 0.0 copy-start.5
  3.8 20.0 %all-to-all-start = ((bf16[128,32,128]{2,1,0:T(8,128)(2,1)}), bf16[128,32,128]{2,1,0:T(8,128)(2,1)S(1)}, u32[]{:S(2)}, u32[]{:S(2)}) async-start(bf16[128,32,128]{2,1,0:T(8,128)(2,1)} %shard_map.94), calls=%async_computation | async-start | bytes 2097152 | tf_op jit(solution)/shard_map/all_to_all | solution.py:188
  23.7 0.0 copy-done.5
  23.7 0.1 copy.14
  23.8 0.0 copy-start.2
  23.8 0.0 copy-start.3
  23.8 1.1 %pad_maximum_fusion.far_hbm = bf16[128,32,128]{2,1,0:T(8,128)(2,1)} fusion(bf16[64,32,128]{2,1,0:T(8,128)(2,1)S(1)} %bitcast.21), kind=kLoop, calls=%fused_computation | loop fusion | flops 524288 | bytes 1572864 | tf_op jit(solution)/shard_map/concatenate | solution.py:66
  24.9 31.3 %all-to-all-done.in_ref = bf16[128,32,128]{2,1,0:T(8,128)(2,1)S(1)} async-done(((bf16[128,32,128]{2,1,0:T(8,128)(2,1)}), bf16[128,32,128]{2,1,0:T(8,128)(2,1)S(1)}, u32[]{:S(2)}, u32[]{:S(2)}) %all-to-all-start) | async-done | bytes 1048608 | tf_op jit(solution)/shard_map/all_to_all | solution.py:188
  56.3 0.0 copy-done.2
  56.3 2.9 %shard_map.95 = (bf16[128,32,128]{2,1,0:T(8,128)(2,1)}, f32[4,512,128]{2,1,0:T(8,128)S(1)}) custom-call(bf16[128,32,128]{2,1,0:T(8,128)(2,1)S(1)} %all-to-all-done.in_ref, bf16[512,512]{1,0:T(8,128)(2,1)S(1)} %copy-done.2, bf16[512,512]{1,0:T(8,128)(2,1)S(1)} %copy-done.3, bf16[128,32,128]{2,1,0:T(8,128)(2,1)} %pad_maximum_fusion.far_hbm), custom_call_target="tpu_custom_call", output_to_operand_aliasing={{0}: (3, {})} | custom-call | flops 1073741824 | bytes 4194304 | tf_op jit(solution)/shard_map/pallas_call | solution.py:127
  59.1 6.5 %all-to-all-start.1 = ((bf16[128,32,128]{2,1,0:T(8,128)(2,1)}), bf16[128,32,128]{2,1,0:T(8,128)(2,1)S(1)}, u32[]{:S(2)}, u32[]{:S(2)}) async-start(bf16[128,32,128]{2,1,0:T(8,128)(2,1)} %get-tuple-element.7), calls=%async_computation.1 | async-start | bytes 2097152 | tf_op jit(solution)/shard_map/all_to_all | solution.py:191
  65.7 0.3 copy.15
  66.1 1.9 %collective-permute-start = (bf16[4,512,2,32]{1,3,2,0:T(8,128)(2,1)S(1)}, bf16[4,512,2,32]{1,3,2,0:T(8,128)(2,1)S(1)}, u32[]{:S(2)}, u32[]{:S(2)}) collective-permute-start(bf16[4,512,2,32]{1,3,2,0:T(8,128)(2,1)S(1)} %fusion), channel_id=1, source_target_pairs={{0,1},{1,0},{2,3},{3,2},{4,5},{5,4},{6,7},{7,6},{8,9},{9,8},{10,11... | collective-permute-start | bytes 786440 | tf_op jit(solution)/shard_map/ppermute | solution.py:174
  68.0 1.5 %collective-permute-done = bf16[4,512,2,32]{1,3,2,0:T(8,128)(2,1)S(1)} collective-permute-done((bf16[4,512,2,32]{1,3,2,0:T(8,128)(2,1)S(1)}, bf16[4,512,2,32]{1,3,2,0:T(8,128)(2,1)S(1)}, u32[]{:S(2)}, u32[]{:S(2)}) %collective-permute-start) | collective-permute-done | bytes 262176 | tf_op jit(solution)/shard_map/ppermute | solution.py:174
  69.5 0.1 bitcast_add_fusion
  69.6 0.0 copy-start.4
  69.6 0.8 copy-done.4
  70.4 2.6 %collective-permute-start.1 = (bf16[4,512,32]{1,2,0:T(8,128)(2,1)S(1)}, bf16[4,512,32]{1,2,0:T(8,128)(2,1)S(1)}, u32[]{:S(2)}, u32[]{:S(2)}) collective-permute-start(bf16[4,512,32]{1,2,0:T(8,128)(2,1)S(1)} %fusion.2), channel_id=1, source_target_pairs={{0,2},{2,0},{1,3},{3,1},{4,6},{6,4},{5,7},{7,5},{8,10},{10,8},{9,1... | collective-permute-start | bytes 393224 | tf_op jit(solution)/shard_map/ppermute | solution.py:178
  73.1 6.7 %collective-permute-done.1 = bf16[4,512,32]{1,2,0:T(8,128)(2,1)S(1)} collective-permute-done((bf16[4,512,32]{1,2,0:T(8,128)(2,1)S(1)}, bf16[4,512,32]{1,2,0:T(8,128)(2,1)S(1)}, u32[]{:S(2)}, u32[]{:S(2)}) %collective-permute-start.1) | collective-permute-done | bytes 131104 | tf_op jit(solution)/shard_map/ppermute | solution.py:178
  79.8 1.7 %fusion.1 = f32[512,4,32]{0,2,1:T(8,128)} fusion(bf16[4,512,32]{1,2,0:T(8,128)(2,1)S(1)} %collective-permute-done.1, f32[4,512,2,32]{1,3,2,0:T(8,128)} %copy-done.4, s32[]{:T(128)S(6)} %select_n.16), kind=kLoop, calls=%fused_computation.5 | loop fusion | flops 131072 | bytes 655364 | tf_op jit(solution)/shard_map/transpose | solution.py:179
  81.5 16.2 %all-to-all-done.1.in_ref = bf16[128,32,128]{2,1,0:T(8,128)(2,1)S(1)} async-done(((bf16[128,32,128]{2,1,0:T(8,128)(2,1)}), bf16[128,32,128]{2,1,0:T(8,128)(2,1)S(1)}, u32[]{:S(2)}, u32[]{:S(2)}) %all-to-all-start.1) | async-done | bytes 1048608 | tf_op jit(solution)/shard_map/all_to_all | solution.py:191
  97.7 0.0 copy-done
  97.7 1.6 %shard_map.96 = (bf16[2048,128]{1,0:T(8,128)(2,1)}, bf16[2048,128]{1,0:T(8,128)(2,1)}) custom-call(bf16[128,32,128]{2,1,0:T(8,128)(2,1)S(1)} %all-to-all-done.1.in_ref, bf16[512,512]{1,0:T(8,128)(2,1)S(1)} %copy-done.1, bf16[512,512]{1,0:T(8,128)(2,1)S(1)} %copy-done), custom_call_target="tpu_custom_call" | custom-call | flops 536870912 | bytes 4194304 | tf_op jit(solution)/shard_map/pallas_call | solution.py:127
  (6 shorter events, 0.1 us)
Async XLA Ops:
  3.7 20.0 %copy-start.5 = (bf16[512,4,128]{2,1,0:T(4,128)(2,1)S(1)}, bf16[512,4,128]{2,1,0:T(4,128)(2,1)}, u32[]{:S(2)}) copy-start(bf16[512,4,128]{2,1,0:T(4,128)(2,1)} %param.9) | copy-start | bytes 1572868
  3.8 52.5 %all-to-all-start = ((bf16[128,32,128]{2,1,0:T(8,128)(2,1)}), bf16[128,32,128]{2,1,0:T(8,128)(2,1)S(1)}, u32[]{:S(2)}, u32[]{:S(2)}) async-start(bf16[128,32,128]{2,1,0:T(8,128)(2,1)} %shard_map.94), calls=%async_computation | async-start | bytes 2097152 | tf_op jit(solution)/shard_map/all_to_all | solution.py:188
  23.8 32.4 %copy-start.2 = (bf16[512,512]{1,0:T(8,128)(2,1)S(1)}, bf16[512,512]{1,0:T(8,128)(2,1)}, u32[]{:S(2)}) copy-start(bf16[512,512]{1,0:T(8,128)(2,1)} %mix.2) | copy-start | bytes 1572868
  23.8 32.4 %copy-start.3 = (bf16[512,512]{1,0:T(8,128)(2,1)S(1)}, bf16[512,512]{1,0:T(8,128)(2,1)}, u32[]{:S(2)}) copy-start(bf16[512,512]{1,0:T(8,128)(2,1)} %unmix.2) | copy-start | bytes 1572868
  59.1 38.6 %all-to-all-start.1 = ((bf16[128,32,128]{2,1,0:T(8,128)(2,1)}), bf16[128,32,128]{2,1,0:T(8,128)(2,1)S(1)}, u32[]{:S(2)}, u32[]{:S(2)}) async-start(bf16[128,32,128]{2,1,0:T(8,128)(2,1)} %get-tuple-element.7), calls=%async_computation.1 | async-start | bytes 2097152 | tf_op jit(solution)/shard_map/all_to_all | solution.py:191
  66.1 3.4 %collective-permute-start = (bf16[4,512,2,32]{1,3,2,0:T(8,128)(2,1)S(1)}, bf16[4,512,2,32]{1,3,2,0:T(8,128)(2,1)S(1)}, u32[]{:S(2)}, u32[]{:S(2)}) collective-permute-start(bf16[4,512,2,32]{1,3,2,0:T(8,128)(2,1)S(1)} %fusion), channel_id=1, source_target_pairs={{0,1},{1,0},{2,3},{3,2},{4,5},{5,4},{6,7},{7,6},{8,9},{9,8},{10,11... | collective-permute-start | bytes 786440 | tf_op jit(solution)/shard_map/ppermute | solution.py:174
  69.5 28.2 %copy-start.1 = (bf16[512,512]{1,0:T(8,128)(2,1)S(1)}, bf16[512,512]{1,0:T(8,128)(2,1)}, u32[]{:S(2)}) copy-start(bf16[512,512]{1,0:T(8,128)(2,1)} %unmix.3) | copy-start | bytes 1572868
  69.6 0.8 copy-start.4
  70.4 27.3 %copy-start = (bf16[512,512]{1,0:T(8,128)(2,1)S(1)}, bf16[512,512]{1,0:T(8,128)(2,1)}, u32[]{:S(2)}) copy-start(bf16[512,512]{1,0:T(8,128)(2,1)} %mix.3) | copy-start | bytes 1572868
  70.4 9.4 %collective-permute-start.1 = (bf16[4,512,32]{1,2,0:T(8,128)(2,1)S(1)}, bf16[4,512,32]{1,2,0:T(8,128)(2,1)S(1)}, u32[]{:S(2)}, u32[]{:S(2)}) collective-permute-start(bf16[4,512,32]{1,2,0:T(8,128)(2,1)S(1)} %fusion.2), channel_id=1, source_target_pairs={{0,2},{2,0},{1,3},{3,1},{4,6},{6,4},{5,7},{7,5},{8,10},{10,8},{9,1... | collective-permute-start | bytes 393224 | tf_op jit(solution)/shard_map/ppermute | solution.py:178

commit v5 on v4

v5 whole, which is shorter than its diff:
```python
import functools

import jax
import jax.numpy as jnp
from jax import lax
from jax.experimental import pallas as pl
from jax.experimental.pallas import tpu as pltpu
from jax.sharding import PartitionSpec as P

SUBLANES = 8
HALVES = 2
WHOLE_VMEM = 62 * 1024 * 1024
MOST_VMEM = 24 * 1024 * 1024


def dot(left, right, left_dim=1):
    return lax.dot_general(left, right, (((left_dim,), (0,)), ((), ())), preferred_element_type=jnp.float32)


class Copies:
    def __init__(self, sems):
        self.sems, self.started = sems, []

    def start(self, src, dst):
        copy = pltpu.make_async_copy(src, dst, self.sems.at[len(self.started)])
        copy.start()
        self.started.append(copy)
        return copy


def halves(block):
    return [slice(h * (block // HALVES), (h + 1) * (block // HALVES)) for h in range(HALVES)]


def rows_of(weight, left_dim, cut):
    return weight[:, cut] if left_dim == 0 else weight[cut, :]


def send_product(slab, weight, left_dim, right, stage, out_buf, out_ref, part, copies):
    block, width = right.shape
    channels = width // slab
    rows = slab * slab
    here = pl.ds(part * rows, rows)
    given = []
    for cut in halves(block):
        product = dot(rows_of(weight, left_dim, cut), right, left_dim)
        height = cut.stop - cut.start
        for g in range(slab):
            stage[pl.ds(cut.start * slab + g, height, stride=slab), :] = product[:, g * channels : (g + 1) * channels]
        groups = pl.ds(cut.start // slab, height // slab)
        ready = stage[pl.ds(cut.start * slab, height * slab), :].astype(jnp.bfloat16)
        out_buf[groups, here, :] = ready.reshape(height // slab, rows, channels)
        given.append(copies.start(out_buf.at[groups, here], out_ref.at[groups, here]))
    return given


def gather_rows(slab, in_ref, part):
    groups, _, channels = in_ref.shape
    rows = slab * slab
    tiles = rows // SUBLANES
    got = in_ref[:, part * rows : (part + 1) * rows, :].astype(jnp.float32)
    got = got.reshape(groups // 2, 2, tiles, SUBLANES, channels)
    turned = pltpu.roll(got.reshape(groups * tiles, SUBLANES, channels), slab, axis=1).reshape(got.shape)
    low = lax.broadcasted_iota(jnp.int32, (groups // 2, tiles, SUBLANES, channels), 2) < slab
    even = jnp.where(low, got[:, 0], turned[:, 1]).astype(jnp.bfloat16)
    odd = jnp.where(low, turned[:, 0], got[:, 1]).astype(jnp.bfloat16)
    lanes = [half[:, t].reshape(groups * slab, channels) for t in range(tiles) for half in (even, odd)]
    return jnp.concatenate(lanes, axis=1)


def lanes_of(ref, slab):
    block = ref.shape[0] // slab
    return jnp.concatenate([ref[a * block : (a + 1) * block, :] for a in range(slab)], axis=1)


def before_kernel(slab, tok_hbm, cot_hbm, mix_hbm, unmix_hbm, out_ref, tok, cot, mix, unmix, stage, out_buf, sems):
    copies = Copies(sems)
    got = [copies.start(src, dst) for src, dst in ((mix_hbm, mix), (tok_hbm, tok), (unmix_hbm, unmix), (cot_hbm, cot))]
    given = []
    for part, (weight, data, left_dim) in enumerate(((mix, tok, 0), (unmix, cot, 1))):
        got[2 * part].wait()
        got[2 * part + 1].wait()
        given += send_product(slab, weight, left_dim, lanes_of(data, slab), stage.at[part], out_buf, out_ref, part, copies)
    for copy in given:
        copy.wait()


def between_kernel(slab, in_ref, mix, unmix, ker_hbm, out_ref, term_ref, ker, ker_rows, stage, out_buf, sems):
    block, channels = mix.shape[0], in_ref.shape[2]
    copies = Copies(sems)
    got_ker = copies.start(ker_hbm, ker)
    spectrum = dot(mix[...], gather_rows(slab, in_ref, 0), 0).astype(jnp.bfloat16).astype(jnp.float32)
    gradf = dot(unmix[...], gather_rows(slab, in_ref, 1)).astype(jnp.bfloat16).astype(jnp.float32)
    got_ker.wait()
    ker_rows[...] = ker[...].astype(jnp.float32)
    weight = jnp.concatenate([ker_rows[pl.ds(i, block, stride=slab), :] for i in range(slab)], axis=1)
    filtered = (weight * spectrum).astype(jnp.bfloat16)
    given = send_product(slab, unmix, 0, filtered, stage.at[0], out_buf, out_ref, 0, copies)
    grad_spectrum = (weight * gradf).astype(jnp.bfloat16)
    given += send_product(slab, mix, 1, grad_spectrum, stage.at[1], out_buf, out_ref, 1, copies)
    terms = spectrum * gradf
    for i in range(slab):
        term_ref[i] = terms[:, i * channels : (i + 1) * channels]
    for copy in given:
        copy.wait()


def after_kernel(slab, in_ref, unmix, mix, res_ref, tok_ref, out_buf, sems):
    channels = in_ref.shape[2]
    block = unmix.shape[0]
    copies = Copies(sems)
    given = []
    for part, (weight, left_dim, out_ref) in enumerate(((unmix, 0, res_ref), (mix, 1, tok_ref))):
        arrived = gather_rows(slab, in_ref, part)
        for cut in halves(block):
            product = dot(rows_of(weight, left_dim, cut), arrived, left_dim).astype(jnp.bfloat16)
            here = pl.ds(cut.start, cut.stop - cut.start)
            for i in range(slab):
                out_buf[part, i, here, :] = product[:, i * channels : (i + 1) * channels]
            given.append(copies.start(out_buf.at[part, :, here], out_ref.at[:, here]))
    for copy in given:
        copy.wait()


def call(kernel, outs, out_specs, specs, scratch, copies, limit, flops, aliases, *args):
    return pl.pallas_call(
        kernel,
        out_shape=outs,
        in_specs=[pl.BlockSpec(memory_space=space) for space in specs],
        out_specs=jax.tree.map(lambda space: pl.BlockSpec(memory_space=space), out_specs),
        scratch_shapes=[*scratch, pltpu.SemaphoreType.DMA((copies,))],
        input_output_aliases=aliases,
        compiler_params=pltpu.CompilerParams(vmem_limit_bytes=limit),
        cost_estimate=pl.CostEstimate(flops=flops, bytes_accessed=4 * 1024 * 1024, transcendentals=0),
    )(*args)


def kernels(block, slab, channels):
    local_len, groups = block * slab, block // slab
    bf16, f32 = jnp.bfloat16, jnp.float32
    ANY, VMEM = pl.ANY, pltpu.VMEM
    message = jax.ShapeDtypeStruct((groups, 2 * slab * slab, channels), bf16)
    flat = jax.ShapeDtypeStruct((slab, block, channels), bf16)
    stage = VMEM((2, local_len, channels), f32)
    buffer = VMEM(message.shape, bf16)
    piece, matrix = VMEM((local_len, channels), bf16), VMEM((block, block), bf16)
    flops = 2 * block * block * slab * channels
    before = functools.partial(
        call, functools.partial(before_kernel, slab), message, ANY, [ANY] * 4,
        [piece, piece, matrix, matrix, stage, buffer], 4 + 2 * HALVES, WHOLE_VMEM, 2 * flops, {},
    )
    between = functools.partial(
        call, functools.partial(between_kernel, slab), (message, jax.ShapeDtypeStruct((slab, block, channels), f32)),
        (ANY, VMEM), [VMEM, VMEM, VMEM, ANY],
        [piece, VMEM((local_len, channels), f32), stage, buffer], 1 + 2 * HALVES, MOST_VMEM, 4 * flops, {},
    )
    after = functools.partial(
        call, functools.partial(after_kernel, slab), (flat, flat), (ANY, ANY), [VMEM] * 3,
        [VMEM((2, slab, block, channels), bf16)], 2 * HALVES, MOST_VMEM, 2 * flops, {},
    )
    return before, between, after


def batch_sum(terms):
    inner, outer, channels = terms.shape
    quarter = channels // 4
    place = lax.axis_index("batch")
    core, side = lax.rem(place, 2), lax.div(place, 2)
    parts = terms.reshape(inner, outer, 2, 2, quarter)
    mine = lax.dynamic_index_in_dim(parts, core, 3, keepdims=False)
    other = lax.dynamic_index_in_dim(parts, 1 - core, 3, keepdims=False).astype(jnp.bfloat16)
    got = lax.ppermute(other, "batch", [(0, 1), (1, 0), (2, 3), (3, 2)])
    pair = mine + got.astype(jnp.float32)
    keep = lax.dynamic_index_in_dim(pair, side, 2, keepdims=False)
    give = lax.dynamic_index_in_dim(pair, 1 - side, 2, keepdims=False).astype(jnp.bfloat16)
    got = lax.ppermute(give, "batch", [(0, 2), (2, 0), (1, 3), (3, 1)])
    return (keep + got.astype(jnp.float32)).transpose(1, 0, 2)


def body(tokens, grad_out, kernel, mix_inner, mix_outer, unmix_outer, unmix_inner):
    local_len, channels = tokens.shape[1:]
    block = mix_inner.shape[0]
    slab = local_len // block
    before, between, after = kernels(block, slab, channels)
    sent = before(tokens.reshape(local_len, channels), grad_out.reshape(local_len, channels), mix_inner, unmix_inner)
    here = lax.all_to_all(sent, "seq", split_axis=0, concat_axis=0, tiled=True)
    sent, terms = between(here, mix_outer, unmix_outer, kernel.reshape(local_len, channels))
    back = lax.all_to_all(sent, "seq", split_axis=0, concat_axis=0, tiled=True)
    grad_kernel = batch_sum(terms)
    output, grad_tokens = after(back, unmix_inner, mix_inner)
    return (output.reshape(1, local_len, channels), grad_tokens.reshape(1, local_len, channels), grad_kernel)


def solution(mesh):
    return jax.shard_map(
        body,
        mesh=mesh,
        in_specs=(
            P("batch", "seq", None),
            P("batch", "seq", None),
            P(None, "seq", None),
            P(),
            P(),
            P(),
            P(),
        ),
        out_specs=(P("batch", "seq", None), P("batch", "seq", None), P(None, "seq", "batch")),
        check_vma=False,
    )
```

time: 99.7 us -> 99.2 us (level)
  blocking collectives: 0 us -> 52.5 us
  waiting for transfers between devices: 55.8 us -> 24.4 us
  starting transfers between devices: 31.1 us -> 11.1 us
  other arithmetic: 2.82 us -> 1.76 us
    all_to_all x0 -> x1, blocking collectives: none -> 52.5 us  [body(): here = lax.all_to_all(sent, 'seq', split_axis=0, concat_axis=0, tiled=True)]
    all_to_all x1 -> x0, waiting for transfers between devices: 31.3 us -> none  [body(): here = lax.all_to_all(sent, 'seq', split_axis=0, concat_axis=0, tiled=True)]
    all_to_all x1 -> x0, starting transfers between devices: 20 us -> none  [body(): here = lax.all_to_all(sent, 'seq', split_axis=0, concat_axis=0, tiled=True)]
    concatenate x1 -> x0, other arithmetic: 1.06 us -> none  [far_of(): return jnp.concatenate([rows] * (shape[0] // rows.shape[0]), axis=0)]
  transfers between devices with their start and end apart: 4 -> 3, of which waited for: 4 -> 3; matrix products, arithmetic and copies ran while one was open for 3% -> 2% of each run, Pallas kernels for 0% -> 0%
where the time goes in v5:
time: 99.2 us; the launch traced here: 98.8 us
  blocking collectives  52.5 us (53%)
  waiting for transfers between devices  24.4 us (25%)
  starting transfers between devices  11.1 us (11%)
  Pallas kernels  7.09 us (7%)
  other arithmetic  1.76 us (2%)
  local copies, waits for them, and re-layouts  1.21 us (1%)
    all_to_all x1, blocking collectives, body(): here = lax.all_to_all(sent, 'seq', split_axis=0, concat_axis=0, tiled=True)  52.5 us
    all_to_all x1, waiting for transfers between devices, body(): back = lax.all_to_all(sent, 'seq', split_axis=0, concat_axis=0, tiled=True)  16.1 us
    pallas_call x3, Pallas kernels, call(): pl.pallas_call(kernel, out_shape=outs, in_specs=[pl.BlockSpec(memory_spac...  7.09 us
    ppermute x1, waiting for transfers between devices, batch_sum(): got = lax.ppermute(give, 'batch', [(0, 2), (2, 0), (1, 3), (3, 1)])  6.81 us
    all_to_all x1, starting transfers between devices, body(): back = lax.all_to_all(sent, 'seq', split_axis=0, concat_axis=0, tiled=True)  6.54 us
    ppermute x1, starting transfers between devices, batch_sum(): got = lax.ppermute(give, 'batch', [(0, 2), (2, 0), (1, 3), (3, 1)])  2.63 us
  transfers between devices with their start and end apart: 3, of which 3 were waited for; matrix products, arithmetic and copies ran while one was open for 2% of the time, Pallas kernels for 0%

profile of v5, /device:TPU:8, one launch (start us, length us, event | category | flops | bytes accessed | tf_op | source)
XLA Modules:
  0.0 98.8 jit_solution(12363733014125988545)
XLA Ops:
  0.6 3.0 %shard_map.94 = bf16[128,32,128]{2,1,0:T(8,128)(2,1)} custom-call(bf16[2048,128]{1,0:T(8,128)(2,1)} %bitcast.21, bf16[2048,128]{1,0:T(8,128)(2,1)} %bitcast.22, bf16[512,512]{1,0:T(8,128)(2,1)} %mix.3, bf16[512,512]{1,0:T(8,128)(2,1)} %unmix.3), custom_call_target="tpu_custom_call" | custom-call | flops 536870912 | bytes 4194304 | tf_op jit(solution)/shard_map/pallas_call | solution.py:126
  3.6 0.0 copy-start.2
  3.7 0.0 copy-start.3
  3.7 0.0 copy-start.4
  3.7 52.5 %all_to_all.10.in_ref = bf16[128,32,128]{2,1,0:T(8,128)(2,1)S(1)} all-to-all(bf16[128,32,128]{2,1,0:T(8,128)(2,1)} %shard_map.94), channel_id=1, replica_groups=mesh['seq'=128,'batch'=4] {'seq'}, dimensions={0} | all-to-all | bytes 2097152 | tf_op jit(solution)/shard_map/all_to_all | solution.py:186
  56.2 0.0 copy-done.2
  56.2 0.0 copy-done.3
  56.2 0.0 copy-done.4
  56.2 2.6 %shard_map.95 = (bf16[128,32,128]{2,1,0:T(8,128)(2,1)}, f32[4,512,128]{2,1,0:T(8,128)S(1)}) custom-call(bf16[128,32,128]{2,1,0:T(8,128)(2,1)S(1)} %all_to_all.10.in_ref, bf16[512,512]{1,0:T(8,128)(2,1)S(1)} %copy-done.2, bf16[512,512]{1,0:T(8,128)(2,1)S(1)} %copy-done.3, bf16[2048,128]{1,0:T(8,128)(2,1)S(1)} %bitcast.18), custom_call_target="tpu_custom_call" | custom-call | flops 1073741824 | bytes 4194304 | tf_op jit(solution)/shard_map/pallas_call | solution.py:126
  58.8 6.5 %all-to-all-start.1 = ((bf16[128,32,128]{2,1,0:T(8,128)(2,1)}), bf16[128,32,128]{2,1,0:T(8,128)(2,1)S(1)}, u32[]{:S(2)}, u32[]{:S(2)}) async-start(bf16[128,32,128]{2,1,0:T(8,128)(2,1)} %get-tuple-element.7), calls=%async_computation.1 | async-start | bytes 2097152 | tf_op jit(solution)/shard_map/all_to_all | solution.py:188
  65.3 0.3 copy.12
  65.7 1.9 %collective-permute-start = (bf16[4,512,2,32]{1,3,2,0:T(8,128)(2,1)S(1)}, bf16[4,512,2,32]{1,3,2,0:T(8,128)(2,1)S(1)}, u32[]{:S(2)}, u32[]{:S(2)}) collective-permute-start(bf16[4,512,2,32]{1,3,2,0:T(8,128)(2,1)S(1)} %fusion), channel_id=1, source_target_pairs={{0,1},{1,0},{2,3},{3,2},{4,5},{5,4},{6,7},{7,6},{8,9},{9,8},{10,11... | collective-permute-start | bytes 786440 | tf_op jit(solution)/shard_map/ppermute | solution.py:172
  67.7 1.5 %collective-permute-done = bf16[4,512,2,32]{1,3,2,0:T(8,128)(2,1)S(1)} collective-permute-done((bf16[4,512,2,32]{1,3,2,0:T(8,128)(2,1)S(1)}, bf16[4,512,2,32]{1,3,2,0:T(8,128)(2,1)S(1)}, u32[]{:S(2)}, u32[]{:S(2)}) %collective-permute-start) | collective-permute-done | bytes 262176 | tf_op jit(solution)/shard_map/ppermute | solution.py:172
  69.1 0.0 copy-start.1
  69.1 0.1 bitcast_add_fusion
  69.2 0.0 copy-start.5
  69.2 0.8 copy-done.5
  70.0 2.6 %collective-permute-start.1 = (bf16[4,512,32]{1,2,0:T(8,128)(2,1)S(1)}, bf16[4,512,32]{1,2,0:T(8,128)(2,1)S(1)}, u32[]{:S(2)}, u32[]{:S(2)}) collective-permute-start(bf16[4,512,32]{1,2,0:T(8,128)(2,1)S(1)} %fusion.2), channel_id=1, source_target_pairs={{0,2},{2,0},{1,3},{3,1},{4,6},{6,4},{5,7},{7,5},{8,10},{10,8},{9,1... | collective-permute-start | bytes 393224 | tf_op jit(solution)/shard_map/ppermute | solution.py:176
  72.7 6.8 %collective-permute-done.1 = bf16[4,512,32]{1,2,0:T(8,128)(2,1)S(1)} collective-permute-done((bf16[4,512,32]{1,2,0:T(8,128)(2,1)S(1)}, bf16[4,512,32]{1,2,0:T(8,128)(2,1)S(1)}, u32[]{:S(2)}, u32[]{:S(2)}) %collective-permute-start.1) | collective-permute-done | bytes 131104 | tf_op jit(solution)/shard_map/ppermute | solution.py:176
  79.5 1.7 %fusion.1 = f32[512,4,32]{0,2,1:T(8,128)} fusion(bf16[4,512,32]{1,2,0:T(8,128)(2,1)S(1)} %collective-permute-done.1, f32[4,512,2,32]{1,3,2,0:T(8,128)} %copy-done.5, s32[]{:T(128)S(6)} %select_n.16), kind=kLoop, calls=%fused_computation.4 | loop fusion | flops 131072 | bytes 655364 | tf_op jit(solution)/shard_map/transpose | solution.py:177
  81.2 16.1 %all-to-all-done.1.in_ref = bf16[128,32,128]{2,1,0:T(8,128)(2,1)S(1)} async-done(((bf16[128,32,128]{2,1,0:T(8,128)(2,1)}), bf16[128,32,128]{2,1,0:T(8,128)(2,1)S(1)}, u32[]{:S(2)}, u32[]{:S(2)}) %all-to-all-start.1) | async-done | bytes 1048608 | tf_op jit(solution)/shard_map/all_to_all | solution.py:188
  97.3 0.0 copy-done.1
  97.3 0.0 copy-done
  97.3 1.5 %shard_map.96 = (bf16[4,512,128]{2,1,0:T(8,128)(2,1)}, bf16[4,512,128]{2,1,0:T(8,128)(2,1)}) custom-call(bf16[128,32,128]{2,1,0:T(8,128)(2,1)S(1)} %all-to-all-done.1.in_ref, bf16[512,512]{1,0:T(8,128)(2,1)S(1)} %copy-done.1, bf16[512,512]{1,0:T(8,128)(2,1)S(1)} %copy-done), custom_call_target="tpu_custom_call" | custom-call | flops 536870912 | bytes 4194304 | tf_op jit(solution)/shard_map/pallas_call | solution.py:126
  (3 shorter events, 0.1 us)
Async XLA Ops:
  3.6 52.5 %copy-start.2 = (bf16[512,512]{1,0:T(8,128)(2,1)S(1)}, bf16[512,512]{1,0:T(8,128)(2,1)}, u32[]{:S(2)}) copy-start(bf16[512,512]{1,0:T(8,128)(2,1)} %mix.2) | copy-start | bytes 1572868
  3.7 52.5 %copy-start.3 = (bf16[512,512]{1,0:T(8,128)(2,1)S(1)}, bf16[512,512]{1,0:T(8,128)(2,1)}, u32[]{:S(2)}) copy-start(bf16[512,512]{1,0:T(8,128)(2,1)} %unmix.2) | copy-start | bytes 1572868
  3.7 52.5 %copy-start.4 = (bf16[512,4,128]{2,1,0:T(4,128)(2,1)S(1)}, bf16[512,4,128]{2,1,0:T(4,128)(2,1)}, u32[]{:S(2)}) copy-start(bf16[512,4,128]{2,1,0:T(4,128)(2,1)} %param.9) | copy-start | bytes 1572868
  58.8 38.6 %all-to-all-start.1 = ((bf16[128,32,128]{2,1,0:T(8,128)(2,1)}), bf16[128,32,128]{2,1,0:T(8,128)(2,1)S(1)}, u32[]{:S(2)}, u32[]{:S(2)}) async-start(bf16[128,32,128]{2,1,0:T(8,128)(2,1)} %get-tuple-element.7), calls=%async_computation.1 | async-start | bytes 2097152 | tf_op jit(solution)/shard_map/all_to_all | solution.py:188
  65.7 3.4 %collective-permute-start = (bf16[4,512,2,32]{1,3,2,0:T(8,128)(2,1)S(1)}, bf16[4,512,2,32]{1,3,2,0:T(8,128)(2,1)S(1)}, u32[]{:S(2)}, u32[]{:S(2)}) collective-permute-start(bf16[4,512,2,32]{1,3,2,0:T(8,128)(2,1)S(1)} %fusion), channel_id=1, source_target_pairs={{0,1},{1,0},{2,3},{3,2},{4,5},{5,4},{6,7},{7,6},{8,9},{9,8},{10,11... | collective-permute-start | bytes 786440 | tf_op jit(solution)/shard_map/ppermute | solution.py:172
  69.1 28.2 %copy-start.1 = (bf16[512,512]{1,0:T(8,128)(2,1)S(1)}, bf16[512,512]{1,0:T(8,128)(2,1)}, u32[]{:S(2)}) copy-start(bf16[512,512]{1,0:T(8,128)(2,1)} %unmix.3) | copy-start | bytes 1572868
  69.2 0.8 copy-start.5
  70.0 27.3 %copy-start = (bf16[512,512]{1,0:T(8,128)(2,1)S(1)}, bf16[512,512]{1,0:T(8,128)(2,1)}, u32[]{:S(2)}) copy-start(bf16[512,512]{1,0:T(8,128)(2,1)} %mix.3) | copy-start | bytes 1572868
  70.0 9.5 %collective-permute-start.1 = (bf16[4,512,32]{1,2,0:T(8,128)(2,1)S(1)}, bf16[4,512,32]{1,2,0:T(8,128)(2,1)S(1)}, u32[]{:S(2)}, u32[]{:S(2)}) collective-permute-start(bf16[4,512,32]{1,2,0:T(8,128)(2,1)S(1)} %fusion.2), channel_id=1, source_target_pairs={{0,2},{2,0},{1,3},{3,1},{4,6},{6,4},{5,7},{7,5},{8,10},{10,8},{9,1... | collective-permute-start | bytes 393224 | tf_op jit(solution)/shard_map/ppermute | solution.py:176

commit v6 on v5

--- a/solution.py
+++ b/solution.py
@@ -168,6 +168,47 @@
     core, side = lax.rem(place, 2), lax.div(place, 2)
     parts = terms.reshape(inner, outer, 2, 2, quarter)
     mine = lax.dynamic_index_in_dim(parts, core, 3, keepdims=False)
+    other = lax.dynamic_index_in_dim(parts, 1 - core, 3, keepdims=False)
+    pair = mine + lax.ppermute(other, "batch", [(0, 1), (1, 0), (2, 3), (3, 2)])
+    keep = lax.dynamic_index_in_dim(pair, side, 2, keepdims=False)
+    give = lax.dynamic_index_in_dim(pair, 1 - side, 2, keepdims=False)
+    total = keep + lax.ppermute(give, "batch", [(0, 2), (2, 0), (1, 3), (3, 1)])
+    return total.transpose(1, 0, 2)
+
+
+def kernels(block, slab, channels):
+    local_len, groups = block * slab, block // slab
+    bf16, f32 = jnp.bfloat16, jnp.float32
+    ANY, VMEM = pl.ANY, pltpu.VMEM
+    message = jax.ShapeDtypeStruct((groups, 2 * slab * slab, channels), bf16)
+    flat = jax.ShapeDtypeStruct((slab, block, channels), bf16)
+    stage = VMEM((2, local_len, channels), f32)
+    buffer = VMEM(message.shape, bf16)
+    piece, matrix = VMEM((local_len, channels), bf16), VMEM((block, block), bf16)
+    flops = 2 * block * block * slab * channels
+    before = functools.partial(
+        call, functools.partial(before_kernel, slab), message, ANY, [ANY] * 4,
+        [piece, piece, matrix, matrix, stage, buffer], 4 + 2 * HALVES, WHOLE_VMEM, 2 * flops, {},
+    )
+    between = functools.partial(
+        call, functools.partial(between_kernel, slab), (message, jax.ShapeDtypeStruct((slab, block, channels), f32)),
+        (ANY, VMEM), [VMEM, VMEM, VMEM, ANY],
+        [piece, VMEM((local_len, channels), f32), stage, buffer], 1 + 2 * HALVES, MOST_VMEM, 4 * flops, {},
+    )
+    after = functools.partial(
+        call, functools.partial(after_kernel, slab), (flat, flat), (ANY, ANY), [VMEM] * 3,
+        [VMEM((2, slab, block, channels), bf16)], 2 * HALVES, MOST_VMEM, 2 * flops, {},
+    )
+    return before, between, after
+
+
+def batch_sum(terms):
+    inner, outer, channels = terms.shape
+    quarter = channels // 4
+    place = lax.axis_index("batch")
+    core, side = lax.rem(place, 2), lax.div(place, 2)
+    parts = terms.reshape(inner, outer, 2, 2, quarter)
+    mine = lax.dynamic_index_in_dim(parts, core, 3, keepdims=False)
     other = lax.dynamic_index_in_dim(parts, 1 - core, 3, keepdims=False).astype(jnp.bfloat16)
     got = lax.ppermute(other, "batch", [(0, 1), (1, 0), (2, 3), (3, 2)])
     pair = mine + got.astype(jnp.float32)

time: 99.2 us -> 99.2 us (level)
  no operation moved by 1% of the time
where the time goes in v6:
time: 99.2 us; the launch traced here: 98.8 us
  blocking collectives  52.5 us (53%)
  waiting for transfers between devices  24.4 us (25%)
  starting transfers between devices  11.1 us (11%)
  Pallas kernels  7.09 us (7%)
  other arithmetic  1.76 us (2%)
  local copies, waits for them, and re-layouts  1.21 us (1%)
    all_to_all x1, blocking collectives, body(): here = lax.all_to_all(sent, 'seq', split_axis=0, concat_axis=0, tiled=True)  52.5 us
    all_to_all x1, waiting for transfers between devices, body(): back = lax.all_to_all(sent, 'seq', split_axis=0, concat_axis=0, tiled=True)  16.1 us
    pallas_call x3, Pallas kernels, call(): pl.pallas_call(kernel, out_shape=outs, in_specs=[pl.BlockSpec(memory_spac...  7.09 us
    ppermute x1, waiting for transfers between devices, batch_sum(): got = lax.ppermute(give, 'batch', [(0, 2), (2, 0), (1, 3), (3, 1)])  6.81 us
    all_to_all x1, starting transfers between devices, body(): back = lax.all_to_all(sent, 'seq', split_axis=0, concat_axis=0, tiled=True)  6.54 us
    ppermute x1, starting transfers between devices, batch_sum(): got = lax.ppermute(give, 'batch', [(0, 2), (2, 0), (1, 3), (3, 1)])  2.63 us
  transfers between devices with their start and end apart: 3, of which 3 were waited for; matrix products, arithmetic and copies ran while one was open for 2% of the time, Pallas kernels for 0%

profile of v6, /device:TPU:8, one launch (start us, length us, event | category | flops | bytes accessed | tf_op | source)
XLA Modules:
  0.0 98.8 jit_solution(12363733014125988545)
XLA Ops:
  0.6 3.0 %shard_map.94 = bf16[128,32,128]{2,1,0:T(8,128)(2,1)} custom-call(bf16[2048,128]{1,0:T(8,128)(2,1)} %bitcast.21, bf16[2048,128]{1,0:T(8,128)(2,1)} %bitcast.22, bf16[512,512]{1,0:T(8,128)(2,1)} %mix.3, bf16[512,512]{1,0:T(8,128)(2,1)} %unmix.3), custom_call_target="tpu_custom_call" | custom-call | flops 536870912 | bytes 4194304 | tf_op jit(solution)/shard_map/pallas_call | solution.py:126
  3.6 0.0 copy-start.2
  3.7 0.0 copy-start.3
  3.7 0.0 copy-start.4
  3.7 52.5 %all_to_all.10.in_ref = bf16[128,32,128]{2,1,0:T(8,128)(2,1)S(1)} all-to-all(bf16[128,32,128]{2,1,0:T(8,128)(2,1)} %shard_map.94), channel_id=1, replica_groups=mesh['seq'=128,'batch'=4] {'seq'}, dimensions={0} | all-to-all | bytes 2097152 | tf_op jit(solution)/shard_map/all_to_all | solution.py:227
  56.2 0.0 copy-done.2
  56.2 0.0 copy-done.3
  56.2 0.0 copy-done.4
  56.2 2.6 %shard_map.95 = (bf16[128,32,128]{2,1,0:T(8,128)(2,1)}, f32[4,512,128]{2,1,0:T(8,128)S(1)}) custom-call(bf16[128,32,128]{2,1,0:T(8,128)(2,1)S(1)} %all_to_all.10.in_ref, bf16[512,512]{1,0:T(8,128)(2,1)S(1)} %copy-done.2, bf16[512,512]{1,0:T(8,128)(2,1)S(1)} %copy-done.3, bf16[2048,128]{1,0:T(8,128)(2,1)S(1)} %bitcast.18), custom_call_target="tpu_custom_call" | custom-call | flops 1073741824 | bytes 4194304 | tf_op jit(solution)/shard_map/pallas_call | solution.py:126
  58.8 6.5 %all-to-all-start.1 = ((bf16[128,32,128]{2,1,0:T(8,128)(2,1)}), bf16[128,32,128]{2,1,0:T(8,128)(2,1)S(1)}, u32[]{:S(2)}, u32[]{:S(2)}) async-start(bf16[128,32,128]{2,1,0:T(8,128)(2,1)} %get-tuple-element.7), calls=%async_computation.1 | async-start | bytes 2097152 | tf_op jit(solution)/shard_map/all_to_all | solution.py:229
  65.3 0.3 copy.12
  65.7 1.9 %collective-permute-start = (bf16[4,512,2,32]{1,3,2,0:T(8,128)(2,1)S(1)}, bf16[4,512,2,32]{1,3,2,0:T(8,128)(2,1)S(1)}, u32[]{:S(2)}, u32[]{:S(2)}) collective-permute-start(bf16[4,512,2,32]{1,3,2,0:T(8,128)(2,1)S(1)} %fusion), channel_id=1, source_target_pairs={{0,1},{1,0},{2,3},{3,2},{4,5},{5,4},{6,7},{7,6},{8,9},{9,8},{10,11... | collective-permute-start | bytes 786440 | tf_op jit(solution)/shard_map/ppermute | solution.py:213
  67.7 1.5 %collective-permute-done = bf16[4,512,2,32]{1,3,2,0:T(8,128)(2,1)S(1)} collective-permute-done((bf16[4,512,2,32]{1,3,2,0:T(8,128)(2,1)S(1)}, bf16[4,512,2,32]{1,3,2,0:T(8,128)(2,1)S(1)}, u32[]{:S(2)}, u32[]{:S(2)}) %collective-permute-start) | collective-permute-done | bytes 262176 | tf_op jit(solution)/shard_map/ppermute | solution.py:213
  69.1 0.0 copy-start.1
  69.1 0.1 bitcast_add_fusion
  69.2 0.0 copy-start.5
  69.2 0.8 copy-done.5
  70.0 2.6 %collective-permute-start.1 = (bf16[4,512,32]{1,2,0:T(8,128)(2,1)S(1)}, bf16[4,512,32]{1,2,0:T(8,128)(2,1)S(1)}, u32[]{:S(2)}, u32[]{:S(2)}) collective-permute-start(bf16[4,512,32]{1,2,0:T(8,128)(2,1)S(1)} %fusion.2), channel_id=1, source_target_pairs={{0,2},{2,0},{1,3},{3,1},{4,6},{6,4},{5,7},{7,5},{8,10},{10,8},{9,1... | collective-permute-start | bytes 393224 | tf_op jit(solution)/shard_map/ppermute | solution.py:217
  72.7 6.8 %collective-permute-done.1 = bf16[4,512,32]{1,2,0:T(8,128)(2,1)S(1)} collective-permute-done((bf16[4,512,32]{1,2,0:T(8,128)(2,1)S(1)}, bf16[4,512,32]{1,2,0:T(8,128)(2,1)S(1)}, u32[]{:S(2)}, u32[]{:S(2)}) %collective-permute-start.1) | collective-permute-done | bytes 131104 | tf_op jit(solution)/shard_map/ppermute | solution.py:217
  79.5 1.7 %fusion.1 = f32[512,4,32]{0,2,1:T(8,128)} fusion(bf16[4,512,32]{1,2,0:T(8,128)(2,1)S(1)} %collective-permute-done.1, f32[4,512,2,32]{1,3,2,0:T(8,128)} %copy-done.5, s32[]{:T(128)S(6)} %select_n.16), kind=kLoop, calls=%fused_computation.4 | loop fusion | flops 131072 | bytes 655364 | tf_op jit(solution)/shard_map/transpose | solution.py:218
  81.2 16.1 %all-to-all-done.1.in_ref = bf16[128,32,128]{2,1,0:T(8,128)(2,1)S(1)} async-done(((bf16[128,32,128]{2,1,0:T(8,128)(2,1)}), bf16[128,32,128]{2,1,0:T(8,128)(2,1)S(1)}, u32[]{:S(2)}, u32[]{:S(2)}) %all-to-all-start.1) | async-done | bytes 1048608 | tf_op jit(solution)/shard_map/all_to_all | solution.py:229
  97.3 0.0 copy-done.1
  97.3 0.0 copy-done
  97.3 1.5 %shard_map.96 = (bf16[4,512,128]{2,1,0:T(8,128)(2,1)}, bf16[4,512,128]{2,1,0:T(8,128)(2,1)}) custom-call(bf16[128,32,128]{2,1,0:T(8,128)(2,1)S(1)} %all-to-all-done.1.in_ref, bf16[512,512]{1,0:T(8,128)(2,1)S(1)} %copy-done.1, bf16[512,512]{1,0:T(8,128)(2,1)S(1)} %copy-done), custom_call_target="tpu_custom_call" | custom-call | flops 536870912 | bytes 4194304 | tf_op jit(solution)/shard_map/pallas_call | solution.py:126
  (3 shorter events, 0.1 us)
Async XLA Ops:
  3.6 52.5 %copy-start.2 = (bf16[512,512]{1,0:T(8,128)(2,1)S(1)}, bf16[512,512]{1,0:T(8,128)(2,1)}, u32[]{:S(2)}) copy-start(bf16[512,512]{1,0:T(8,128)(2,1)} %mix.2) | copy-start | bytes 1572868
  3.7 52.5 %copy-start.3 = (bf16[512,512]{1,0:T(8,128)(2,1)S(1)}, bf16[512,512]{1,0:T(8,128)(2,1)}, u32[]{:S(2)}) copy-start(bf16[512,512]{1,0:T(8,128)(2,1)} %unmix.2) | copy-start | bytes 1572868
  3.7 52.5 %copy-start.4 = (bf16[512,4,128]{2,1,0:T(4,128)(2,1)S(1)}, bf16[512,4,128]{2,1,0:T(4,128)(2,1)}, u32[]{:S(2)}) copy-start(bf16[512,4,128]{2,1,0:T(4,128)(2,1)} %param.9) | copy-start | bytes 1572868
  58.8 38.6 %all-to-all-start.1 = ((bf16[128,32,128]{2,1,0:T(8,128)(2,1)}), bf16[128,32,128]{2,1,0:T(8,128)(2,1)S(1)}, u32[]{:S(2)}, u32[]{:S(2)}) async-start(bf16[128,32,128]{2,1,0:T(8,128)(2,1)} %get-tuple-element.7), calls=%async_computation.1 | async-start | bytes 2097152 | tf_op jit(solution)/shard_map/all_to_all | solution.py:229
  65.7 3.4 %collective-permute-start = (bf16[4,512,2,32]{1,3,2,0:T(8,128)(2,1)S(1)}, bf16[4,512,2,32]{1,3,2,0:T(8,128)(2,1)S(1)}, u32[]{:S(2)}, u32[]{:S(2)}) collective-permute-start(bf16[4,512,2,32]{1,3,2,0:T(8,128)(2,1)S(1)} %fusion), channel_id=1, source_target_pairs={{0,1},{1,0},{2,3},{3,2},{4,5},{5,4},{6,7},{7,6},{8,9},{9,8},{10,11... | collective-permute-start | bytes 786440 | tf_op jit(solution)/shard_map/ppermute | solution.py:213
  69.1 28.2 %copy-start.1 = (bf16[512,512]{1,0:T(8,128)(2,1)S(1)}, bf16[512,512]{1,0:T(8,128)(2,1)}, u32[]{:S(2)}) copy-start(bf16[512,512]{1,0:T(8,128)(2,1)} %unmix.3) | copy-start | bytes 1572868
  69.2 0.8 copy-start.5
  70.0 27.3 %copy-start = (bf16[512,512]{1,0:T(8,128)(2,1)S(1)}, bf16[512,512]{1,0:T(8,128)(2,1)}, u32[]{:S(2)}) copy-start(bf16[512,512]{1,0:T(8,128)(2,1)} %mix.3) | copy-start | bytes 1572868
  70.0 9.5 %collective-permute-start.1 = (bf16[4,512,32]{1,2,0:T(8,128)(2,1)S(1)}, bf16[4,512,32]{1,2,0:T(8,128)(2,1)S(1)}, u32[]{:S(2)}, u32[]{:S(2)}) collective-permute-start(bf16[4,512,32]{1,2,0:T(8,128)(2,1)S(1)} %fusion.2), channel_id=1, source_target_pairs={{0,2},{2,0},{1,3},{3,1},{4,6},{6,4},{5,7},{7,5},{8,10},{10,8},{9,1... | collective-permute-start | bytes 393224 | tf_op jit(solution)/shard_map/ppermute | solution.py:217

commit v7 on v5

--- a/solution.py
+++ b/solution.py
@@ -168,13 +168,12 @@
     core, side = lax.rem(place, 2), lax.div(place, 2)
     parts = terms.reshape(inner, outer, 2, 2, quarter)
     mine = lax.dynamic_index_in_dim(parts, core, 3, keepdims=False)
-    other = lax.dynamic_index_in_dim(parts, 1 - core, 3, keepdims=False).astype(jnp.bfloat16)
-    got = lax.ppermute(other, "batch", [(0, 1), (1, 0), (2, 3), (3, 2)])
-    pair = mine + got.astype(jnp.float32)
+    other = lax.dynamic_index_in_dim(parts, 1 - core, 3, keepdims=False)
+    pair = mine + lax.ppermute(other, "batch", [(0, 1), (1, 0), (2, 3), (3, 2)])
     keep = lax.dynamic_index_in_dim(pair, side, 2, keepdims=False)
-    give = lax.dynamic_index_in_dim(pair, 1 - side, 2, keepdims=False).astype(jnp.bfloat16)
-    got = lax.ppermute(give, "batch", [(0, 2), (2, 0), (1, 3), (3, 1)])
-    return (keep + got.astype(jnp.float32)).transpose(1, 0, 2)
+    give = lax.dynamic_index_in_dim(pair, 1 - side, 2, keepdims=False)
+    total = keep + lax.ppermute(give, "batch", [(0, 2), (2, 0), (1, 3), (3, 1)])
+    return total.transpose(1, 0, 2)
 
 
 def body(tokens, grad_out, kernel, mix_inner, mix_outer, unmix_outer, unmix_inner):

time: 99.2 us -> 99.2 us (level)
    all_to_all x1, waiting for transfers between devices: 16.1 us -> 10.6 us  [body(): back = lax.all_to_all(sent, 'seq', split_axis=0, concat_axis=0, tiled=True)]
    ppermute x2, waiting for transfers between devices: 8.3 us -> 13.8 us  [the longest x1 11.9 us: batch_sum(): total = keep + lax.ppermute(give, 'batch', [(0, 2), (2, 0), (1, 3), (3, 1)])]
where the time goes in v7:
time: 99.2 us; the launch traced here: 98.8 us
  blocking collectives  52.5 us (53%)
  waiting for transfers between devices  24.4 us (25%)
  starting transfers between devices  11.1 us (11%)
  Pallas kernels  7.09 us (7%)
  other arithmetic  1.77 us (2%)
  local copies, waits for them, and re-layouts  1.21 us (1%)
    all_to_all x1, blocking collectives, body(): here = lax.all_to_all(sent, 'seq', split_axis=0, concat_axis=0, tiled=True)  52.5 us
    ppermute x1, waiting for transfers between devices, batch_sum(): total = keep + lax.ppermute(give, 'batch', [(0, 2), (2, 0), (1, 3), (3, 1)])  11.9 us
    all_to_all x1, waiting for transfers between devices, body(): back = lax.all_to_all(sent, 'seq', split_axis=0, concat_axis=0, tiled=True)  10.6 us
    pallas_call x3, Pallas kernels, call(): pl.pallas_call(kernel, out_shape=outs, in_specs=[pl.BlockSpec(memory_spac...  7.09 us
    all_to_all x1, starting transfers between devices, body(): back = lax.all_to_all(sent, 'seq', split_axis=0, concat_axis=0, tiled=True)  6.54 us
    ppermute x1, starting transfers between devices, batch_sum(): total = keep + lax.ppermute(give, 'batch', [(0, 2), (2, 0), (1, 3), (3, 1)])  2.63 us
  transfers between devices with their start and end apart: 3, of which 3 were waited for; matrix products, arithmetic and copies ran while one was open for 2% of the time, Pallas kernels for 0%

profile of v7, /device:TPU:8, one launch (start us, length us, event | category | flops | bytes accessed | tf_op | source)
XLA Modules:
  0.0 98.8 jit_solution(12921052120214085506)
XLA Ops:
  0.6 3.0 %shard_map.94 = bf16[128,32,128]{2,1,0:T(8,128)(2,1)} custom-call(bf16[2048,128]{1,0:T(8,128)(2,1)} %bitcast.21, bf16[2048,128]{1,0:T(8,128)(2,1)} %bitcast.22, bf16[512,512]{1,0:T(8,128)(2,1)} %mix.3, bf16[512,512]{1,0:T(8,128)(2,1)} %unmix.3), custom_call_target="tpu_custom_call" | custom-call | flops 536870912 | bytes 4194304 | tf_op jit(solution)/shard_map/pallas_call | solution.py:126
  3.6 0.0 copy-start.2
  3.7 0.0 copy-start.3
  3.7 0.0 copy-start.4
  3.7 52.5 %all_to_all.10.in_ref = bf16[128,32,128]{2,1,0:T(8,128)(2,1)S(1)} all-to-all(bf16[128,32,128]{2,1,0:T(8,128)(2,1)} %shard_map.94), channel_id=1, replica_groups=mesh['seq'=128,'batch'=4] {'seq'}, dimensions={0} | all-to-all | bytes 2097152 | tf_op jit(solution)/shard_map/all_to_all | solution.py:185
  56.2 0.0 copy-done.2
  56.2 0.0 copy-done.3
  56.2 0.0 copy-done.4
  56.2 2.6 %shard_map.95 = (bf16[128,32,128]{2,1,0:T(8,128)(2,1)}, f32[4,512,128]{2,1,0:T(8,128)S(1)}) custom-call(bf16[128,32,128]{2,1,0:T(8,128)(2,1)S(1)} %all_to_all.10.in_ref, bf16[512,512]{1,0:T(8,128)(2,1)S(1)} %copy-done.2, bf16[512,512]{1,0:T(8,128)(2,1)S(1)} %copy-done.3, bf16[2048,128]{1,0:T(8,128)(2,1)S(1)} %bitcast.18), custom_call_target="tpu_custom_call" | custom-call | flops 1073741824 | bytes 4194304 | tf_op jit(solution)/shard_map/pallas_call | solution.py:126
  58.8 6.5 %all-to-all-start.1 = ((bf16[128,32,128]{2,1,0:T(8,128)(2,1)}), bf16[128,32,128]{2,1,0:T(8,128)(2,1)S(1)}, u32[]{:S(2)}, u32[]{:S(2)}) async-start(bf16[128,32,128]{2,1,0:T(8,128)(2,1)} %get-tuple-element.7), calls=%async_computation.1 | async-start | bytes 2097152 | tf_op jit(solution)/shard_map/all_to_all | solution.py:187
  65.3 0.3 copy.10
  65.7 1.9 %collective-permute-start = (f32[4,512,2,32]{1,3,2,0:T(8,128)S(1)}, f32[4,512,2,32]{1,3,2,0:T(8,128)S(1)}, u32[]{:S(2)}, u32[]{:S(2)}) collective-permute-start(f32[4,512,2,32]{1,3,2,0:T(8,128)S(1)} %dynamic-slice_bitcast_fusion), channel_id=1, source_target_pairs={{0,1},{1,0},{2,3},{3,2},{4,5},{5,4},{6,7},{7,6},{8,9},{9,8},{10,11... | collective-permute-start | bytes 1572872 | tf_op jit(solution)/shard_map/ppermute | solution.py:172
  67.7 1.9 %collective-permute-done = f32[4,512,2,32]{1,3,2,0:T(8,128)S(1)} collective-permute-done((f32[4,512,2,32]{1,3,2,0:T(8,128)S(1)}, f32[4,512,2,32]{1,3,2,0:T(8,128)S(1)}, u32[]{:S(2)}, u32[]{:S(2)}) %collective-permute-start) | collective-permute-done | bytes 524320 | tf_op jit(solution)/shard_map/ppermute | solution.py:172
  69.5 0.1 bitcast_add_fusion
  69.6 0.0 copy-start.5
  69.6 0.8 copy-done.5
  70.4 0.0 copy-start
  70.4 2.6 %collective-permute-start.1 = (f32[4,512,32]{1,2,0:T(8,128)S(1)}, f32[4,512,32]{1,2,0:T(8,128)S(1)}, u32[]{:S(2)}, u32[]{:S(2)}) collective-permute-start(f32[4,512,32]{1,2,0:T(8,128)S(1)} %dynamic-slice_bitcast_fusion.1), channel_id=1, source_target_pairs={{0,2},{2,0},{1,3},{3,1},{4,6},{6,4},{5,7},{7,5},{8,10},{10,8},{9,1... | collective-permute-start | bytes 786440 | tf_op jit(solution)/shard_map/ppermute | solution.py:175
  73.1 11.9 %collective-permute-done.1 = f32[4,512,32]{1,2,0:T(8,128)S(1)} collective-permute-done((f32[4,512,32]{1,2,0:T(8,128)S(1)}, f32[4,512,32]{1,2,0:T(8,128)S(1)}, u32[]{:S(2)}, u32[]{:S(2)}) %collective-permute-start.1) | collective-permute-done | bytes 262176 | tf_op jit(solution)/shard_map/ppermute | solution.py:175
  85.0 1.7 %fusion = f32[512,4,32]{0,2,1:T(8,128)} fusion(f32[4,512,32]{1,2,0:T(8,128)S(1)} %collective-permute-done.1, f32[4,512,2,32]{1,3,2,0:T(8,128)} %copy-done.5, s32[]{:T(128)S(6)} %select_n.16), kind=kLoop, calls=%fused_computation.3 | loop fusion | flops 65536 | bytes 786436 | tf_op jit(solution)/shard_map/transpose | solution.py:176
  86.7 10.6 %all-to-all-done.1.in_ref = bf16[128,32,128]{2,1,0:T(8,128)(2,1)S(1)} async-done(((bf16[128,32,128]{2,1,0:T(8,128)(2,1)}), bf16[128,32,128]{2,1,0:T(8,128)(2,1)S(1)}, u32[]{:S(2)}, u32[]{:S(2)}) %all-to-all-start.1) | async-done | bytes 1048608 | tf_op jit(solution)/shard_map/all_to_all | solution.py:187
  97.3 0.0 copy-done.1
  97.3 0.0 copy-done
  97.3 1.5 %shard_map.96 = (bf16[4,512,128]{2,1,0:T(8,128)(2,1)}, bf16[4,512,128]{2,1,0:T(8,128)(2,1)}) custom-call(bf16[128,32,128]{2,1,0:T(8,128)(2,1)S(1)} %all-to-all-done.1.in_ref, bf16[512,512]{1,0:T(8,128)(2,1)S(1)} %copy-done.1, bf16[512,512]{1,0:T(8,128)(2,1)S(1)} %copy-done), custom_call_target="tpu_custom_call" | custom-call | flops 536870912 | bytes 4194304 | tf_op jit(solution)/shard_map/pallas_call | solution.py:126
  (3 shorter events, 0.1 us)
Async XLA Ops:
  3.6 52.5 %copy-start.2 = (bf16[512,512]{1,0:T(8,128)(2,1)S(1)}, bf16[512,512]{1,0:T(8,128)(2,1)}, u32[]{:S(2)}) copy-start(bf16[512,512]{1,0:T(8,128)(2,1)} %mix.2) | copy-start | bytes 1572868
  3.7 52.5 %copy-start.3 = (bf16[512,512]{1,0:T(8,128)(2,1)S(1)}, bf16[512,512]{1,0:T(8,128)(2,1)}, u32[]{:S(2)}) copy-start(bf16[512,512]{1,0:T(8,128)(2,1)} %unmix.2) | copy-start | bytes 1572868
  3.7 52.5 %copy-start.4 = (bf16[512,4,128]{2,1,0:T(4,128)(2,1)S(1)}, bf16[512,4,128]{2,1,0:T(4,128)(2,1)}, u32[]{:S(2)}) copy-start(bf16[512,4,128]{2,1,0:T(4,128)(2,1)} %param.9) | copy-start | bytes 1572868
  58.8 38.6 %all-to-all-start.1 = ((bf16[128,32,128]{2,1,0:T(8,128)(2,1)}), bf16[128,32,128]{2,1,0:T(8,128)(2,1)S(1)}, u32[]{:S(2)}, u32[]{:S(2)}) async-start(bf16[128,32,128]{2,1,0:T(8,128)(2,1)} %get-tuple-element.7), calls=%async_computation.1 | async-start | bytes 2097152 | tf_op jit(solution)/shard_map/all_to_all | solution.py:187
  65.7 3.8 %collective-permute-start = (f32[4,512,2,32]{1,3,2,0:T(8,128)S(1)}, f32[4,512,2,32]{1,3,2,0:T(8,128)S(1)}, u32[]{:S(2)}, u32[]{:S(2)}) collective-permute-start(f32[4,512,2,32]{1,3,2,0:T(8,128)S(1)} %dynamic-slice_bitcast_fusion), channel_id=1, source_target_pairs={{0,1},{1,0},{2,3},{3,2},{4,5},{5,4},{6,7},{7,6},{8,9},{9,8},{10,11... | collective-permute-start | bytes 1572872 | tf_op jit(solution)/shard_map/ppermute | solution.py:172
  69.6 0.8 copy-start.5
  70.4 26.9 %copy-start.1 = (bf16[512,512]{1,0:T(8,128)(2,1)S(1)}, bf16[512,512]{1,0:T(8,128)(2,1)}, u32[]{:S(2)}) copy-start(bf16[512,512]{1,0:T(8,128)(2,1)} %unmix.3) | copy-start | bytes 1572868
  70.4 26.9 %copy-start = (bf16[512,512]{1,0:T(8,128)(2,1)S(1)}, bf16[512,512]{1,0:T(8,128)(2,1)}, u32[]{:S(2)}) copy-start(bf16[512,512]{1,0:T(8,128)(2,1)} %mix.3) | copy-start | bytes 1572868
  70.4 14.5 %collective-permute-start.1 = (f32[4,512,32]{1,2,0:T(8,128)S(1)}, f32[4,512,32]{1,2,0:T(8,128)S(1)}, u32[]{:S(2)}, u32[]{:S(2)}) collective-permute-start(f32[4,512,32]{1,2,0:T(8,128)S(1)} %dynamic-slice_bitcast_fusion.1), channel_id=1, source_target_pairs={{0,2},{2,0},{1,3},{3,1},{4,6},{6,4},{5,7},{7,5},{8,10},{10,8},{9,1... | collective-permute-start | bytes 786440 | tf_op jit(solution)/shard_map/ppermute | solution.py:175
